TPU v7x, 32 devices: a whole 2x2x4 slice. The times are simulated.
32 devices in a mesh: section: 2 (over x), dp: 16 (over z, y, core).
Axes of the slice: x: 2, y: 2, z: 4, core: 2. Of those that a mesh axis runs over, the one named last changes fastest.
Arguments:
- inputs: bfloat16 [2, 16, 512, 768], P(None, 'dp'), may hold values from -6 to 6
- segments: int32 [2, 16, 512], P(None, 'dp'), may hold values from 0 to 15, as said below
- cotangent: bfloat16 [2, 16, 512, 768], P(None, 'dp'), may hold values from -6 to 6
- query_weight: bfloat16 [2, 768, 768], P('section'), may hold values from -0.21875 to 0.21875
- query_bias: bfloat16 [2, 768], P('section'), may hold values from -1.75 to 1.75
- key_weight: bfloat16 [2, 768, 768], P('section'), may hold values from -0.21875 to 0.21875
- value_weight: bfloat16 [2, 768, 768], P('section'), may hold values from -0.21875 to 0.21875
- value_bias: bfloat16 [2, 768], P('section'), may hold values from -1.75 to 1.75
- output_weight: bfloat16 [2, 768, 768], P('section'), may hold values from -0.625 to 0.625
- output_bias: bfloat16 [2, 768], P('section'), may hold values from -1.75 to 1.75
- attention_gain: bfloat16 [2, 768], P('section'), may hold values from 0.5 to 1.5
- attention_shift: bfloat16 [2, 768], P('section'), may hold values from -1.75 to 1.75
- inner_weight: bfloat16 [2, 768, 3072], P('section'), may hold values from -0.21875 to 0.21875
- inner_bias: bfloat16 [2, 3072], P('section'), may hold values from -1.75 to 1.75
- outer_weight: bfloat16 [2, 3072, 768], P('section'), may hold values from -0.109375 to 0.109375
- outer_bias: bfloat16 [2, 768], P('section'), may hold values from -1.75 to 1.75
- feed_gain: bfloat16 [2, 768], P('section'), may hold values from 0.5 to 1.5
- feed_shift: bfloat16 [2, 768], P('section'), may hold values from -1.75 to 1.75
Outputs:
- activations: bfloat16 [2, 2, 16, 512, 768], P('section', None, 'dp')
- input_gradients: bfloat16 [2, 2, 16, 512, 768], P('section', None, 'dp')
- query_weight_gradient: float32 [2, 768, 768], P('section')
- query_bias_gradient: float32 [2, 768], P('section')
- key_weight_gradient: float32 [2, 768, 768], P('section')
- value_weight_gradient: float32 [2, 768, 768], P('section')
- value_bias_gradient: float32 [2, 768], P('section')
- output_weight_gradient: float32 [2, 768, 768], P('section')
- output_bias_gradient: float32 [2, 768], P('section')
- attention_gain_gradient: float32 [2, 768], P('section')
- attention_shift_gradient: float32 [2, 768], P('section')
- inner_weight_gradient: float32 [2, 768, 3072], P('section')
- inner_bias_gradient: float32 [2, 3072], P('section')
- outer_weight_gradient: float32 [2, 3072, 768], P('section')
- outer_bias_gradient: float32 [2, 768], P('section')
- feed_gain_gradient: float32 [2, 768], P('section')
- feed_shift_gradient: float32 [2, 768], P('section')
Inputs may be any that keep to these rules, and one draw needn't show every extreme that they name: Along each row the ids never fall; each run of equal ids starts at a multiple of 32 positions and is 1, 4 or 8 times 512 // 16 long; some row holds 16 segments.
All inputs are finite; a program needn't handle non-finite values.
Results may differ from a plain program's by a relative error of at most 0.023.
Values may be sent and summed in bfloat16 or wider, within the bound.
No kernel may reach another device: no remote copies, remote signals or barrier semaphores. Data moves between devices by JAX's collectives and lax.ppermute only.
A program may use at most 320 MiB of HBM per device.

v0:
```python
from functools import partial

import jax
import jax.numpy as jnp
from jax import lax
from jax.sharding import PartitionSpec as P

HEADS = 12
HEAD = 64


def passed_along(value, axis, steps):
    count = lax.axis_size(axis)
    initial, last = (max(0, -steps), min(count, count - steps))
    return lax.ppermute(value, axis, [(source, source + steps) for source in range(initial, last)])


def layer_norm(values_in, norm_gain, norm_shift):
    average = jnp.mean(values_in, axis=-1, keepdims=True)
    centered = values_in - average
    variance = jnp.mean(centered * centered, axis=-1, keepdims=True)
    return centered * lax.rsqrt(variance + 1e-12) * norm_gain + norm_shift


def matmul(left, right):
    return jnp.dot(left, right, preferred_element_type=jnp.float32)


def weight_grad(left, right):
    return jnp.einsum("rld,rlf->df", left, right, preferred_element_type=jnp.float32)


def back_dot(grad_in, weight):
    return jnp.einsum("rlf,df->rld", grad_in, weight, preferred_element_type=jnp.float32)


def row_total(grad_in):
    return jnp.sum(grad_in.astype(jnp.float32), axis=(0, 1))


def scores_of(queries, keys, same_segment):
    scores = jnp.einsum(
        "rqhe,rkhe->rhqk", queries, keys, preferred_element_type=jnp.float32
    ) * HEAD ** (-0.5)
    return jnp.where(same_segment[:, None], scores, -1e30)


def layer_forward(layer_in, same_segment, weights):
    (
        query_weight,
        query_bias,
        key_weight,
        value_weight,
        value_bias,
        output_weight,
        output_bias,
        attention_gain,
        attention_shift,
        inner_weight,
        inner_bias,
        outer_weight,
        outer_bias,
        feed_gain,
        feed_shift,
    ) = weights
    row_count, length = (layer_in.shape[0], layer_in.shape[1])
    queries = (
        (matmul(layer_in, query_weight) + query_bias)
        .astype(jnp.bfloat16)
        .reshape(row_count, length, HEADS, HEAD)
    )
    keys = matmul(layer_in, key_weight).astype(jnp.bfloat16).reshape(row_count, length, HEADS, HEAD)
    values_in = (
        (matmul(layer_in, value_weight) + value_bias)
        .astype(jnp.bfloat16)
        .reshape(row_count, length, HEADS, HEAD)
    )
    scores = scores_of(queries, keys, same_segment)
    top_score = jnp.max(scores, axis=-1, keepdims=True)
    expo = jnp.exp(scores - top_score)
    total = jnp.sum(expo, axis=-1, keepdims=True)
    log_total = top_score + jnp.log(total)
    low_probability = (expo / total).astype(jnp.bfloat16)
    context = jnp.einsum(
        "rhqk,rkhe->rqhe", low_probability, values_in, preferred_element_type=jnp.float32
    )
    context = context.astype(jnp.bfloat16).reshape(row_count, length, HEADS * HEAD)
    branch = matmul(context, output_weight) + output_bias
    pre_attention = layer_in.astype(jnp.float32) + branch
    hidden = layer_norm(pre_attention, attention_gain, attention_shift)
    hidden_low = hidden.astype(jnp.bfloat16)
    inner = matmul(hidden_low, inner_weight) + inner_bias
    activated = jax.nn.gelu(inner, approximate=False).astype(jnp.bfloat16)
    outer = matmul(activated, outer_weight) + outer_bias
    pre_feed = hidden + outer
    result = layer_norm(pre_feed, feed_gain, feed_shift).astype(jnp.bfloat16)
    stored = (
        layer_in,
        queries,
        keys,
        values_in,
        log_total,
        context,
        pre_attention,
        hidden_low,
        inner,
        activated,
        pre_feed,
    )
    return (result, stored)


def layer_backward(grad_out, same_segment, weights, stored):
    (
        query_weight,
        query_bias,
        key_weight,
        value_weight,
        value_bias,
        output_weight,
        output_bias,
        attention_gain,
        attention_shift,
        inner_weight,
        inner_bias,
        outer_weight,
        outer_bias,
        feed_gain,
        feed_shift,
    ) = weights
    (
        layer_in,
        queries,
        keys,
        values_in,
        log_total,
        context,
        pre_attention,
        hidden_low,
        inner,
        activated,
        pre_feed,
    ) = stored
    row_count, length = (layer_in.shape[0], layer_in.shape[1])
    unused, feed_back = jax.vjp(
        layer_norm, pre_feed, feed_gain.astype(jnp.float32), feed_shift.astype(jnp.float32)
    )
    feed_grad, feed_gain_grad, feed_shift_grad = feed_back(grad_out.astype(jnp.float32))
    outer_grad = feed_grad.astype(jnp.bfloat16)
    outer_weight_grad = weight_grad(activated, outer_grad)
    outer_bias_grad = row_total(outer_grad)
    unused, gelu_back = jax.vjp(partial(jax.nn.gelu, approximate=False), inner)
    inner_grad = gelu_back(back_dot(outer_grad, outer_weight))[0].astype(jnp.bfloat16)
    inner_weight_grad = weight_grad(hidden_low, inner_grad)
    inner_bias_grad = row_total(inner_grad)
    hidden_grad = feed_grad + back_dot(inner_grad, inner_weight)
    unused, attention_back = jax.vjp(
        layer_norm,
        pre_attention,
        attention_gain.astype(jnp.float32),
        attention_shift.astype(jnp.float32),
    )
    attention_grad, attention_gain_grad, attention_shift_grad = attention_back(hidden_grad)
    branch_grad = attention_grad.astype(jnp.bfloat16)
    output_weight_grad = weight_grad(context, branch_grad)
    output_bias_grad = row_total(branch_grad)
    context_grad = (
        back_dot(branch_grad, output_weight)
        .astype(jnp.bfloat16)
        .reshape(row_count, length, HEADS, HEAD)
    )
    probability = jnp.exp(scores_of(queries, keys, same_segment) - log_total)
    low_probability = probability.astype(jnp.bfloat16)
    probability_grad = jnp.einsum(
        "rqhe,rkhe->rhqk", context_grad, values_in, preferred_element_type=jnp.float32
    )
    weighted = jnp.sum(probability * probability_grad, axis=-1, keepdims=True)
    score_grad = (probability * (probability_grad - weighted)).astype(jnp.bfloat16)
    query_grad = jnp.einsum(
        "rhqk,rkhe->rqhe", score_grad, keys, preferred_element_type=jnp.float32
    ) * HEAD ** (-0.5)
    query_grad = query_grad.astype(jnp.bfloat16).reshape(row_count, length, HEADS * HEAD)
    key_grad = jnp.einsum(
        "rhqk,rqhe->rkhe", score_grad, queries, preferred_element_type=jnp.float32
    ) * HEAD ** (-0.5)
    key_grad = key_grad.astype(jnp.bfloat16).reshape(row_count, length, HEADS * HEAD)
    value_grad = jnp.einsum(
        "rhqk,rqhe->rkhe", low_probability, context_grad, preferred_element_type=jnp.float32
    )
    value_grad = value_grad.astype(jnp.bfloat16).reshape(row_count, length, HEADS * HEAD)
    layer_grad = (
        attention_grad
        + back_dot(query_grad, query_weight)
        + back_dot(key_grad, key_weight)
        + back_dot(value_grad, value_weight)
    )
    gradients = (
        weight_grad(layer_in, query_grad),
        row_total(query_grad),
        weight_grad(layer_in, key_grad),
        weight_grad(layer_in, value_grad),
        row_total(value_grad),
        output_weight_grad,
        output_bias_grad,
        attention_gain_grad,
        attention_shift_grad,
        inner_weight_grad,
        inner_bias_grad,
        outer_weight_grad,
        outer_bias_grad,
        feed_gain_grad,
        feed_shift_grad,
    )
    return (layer_grad.astype(jnp.bfloat16), gradients)


def pack(gradients):
    small = jnp.concatenate([gradients[member] for member in (1, 4, 6, 7, 8, 12, 13, 14, 10)])
    return (
        gradients[0].reshape(-1),
        gradients[2].reshape(-1),
        gradients[3].reshape(-1),
        gradients[5].reshape(-1),
        gradients[9].reshape(-1),
        gradients[11].reshape(-1),
        small,
    )


def unpack(gathered, width, hidden_width):
    small = gathered[6]
    pieces = [small[index * width : (index + 1) * width] for index in range(8)]
    ordered = (
        gathered[0].reshape(width, width),
        pieces[0],
        gathered[1].reshape(width, width),
        gathered[2].reshape(width, width),
        pieces[1],
        gathered[3].reshape(width, width),
        pieces[2],
        pieces[3],
        pieces[4],
        gathered[4].reshape(width, hidden_width),
        small[8 * width :],
        gathered[5].reshape(hidden_width, width),
        pieces[5],
        pieces[6],
        pieces[7],
    )
    return tuple((member[None] for member in ordered))


def add_tuples(earlier, later):
    if earlier is None:
        return later
    return tuple((left + right for left, right in zip(earlier, later)))


def body(
    inputs,
    segments,
    cotangent,
    query_weight,
    query_bias,
    key_weight,
    value_weight,
    value_bias,
    output_weight,
    output_bias,
    attention_gain,
    attention_shift,
    inner_weight,
    inner_bias,
    outer_weight,
    outer_bias,
    feed_gain,
    feed_shift,
):
    weights = (
        query_weight[0],
        query_bias[0],
        key_weight[0],
        value_weight[0],
        value_bias[0],
        output_weight[0],
        output_bias[0],
        attention_gain[0],
        attention_shift[0],
        inner_weight[0],
        inner_bias[0],
        outer_weight[0],
        outer_bias[0],
        feed_gain[0],
        feed_shift[0],
    )
    section_index = lax.axis_index("section")
    first_section = section_index == 0
    micro_count = inputs.shape[0]
    received = jnp.zeros_like(inputs[0])
    results = []
    stored_steps = []
    for timestep in range(micro_count + 1):
        micro_index = jnp.clip(timestep - section_index, 0, micro_count - 1)
        segment_rows = lax.dynamic_index_in_dim(segments, micro_index, 0, keepdims=False)
        same_segment = segment_rows[:, :, None] == segment_rows[:, None, :]
        layer_in = jnp.where(first_section, inputs[min(timestep, micro_count - 1)], received)
        result, stored = layer_forward(layer_in, same_segment, weights)
        results.append(result)
        stored_steps.append(stored)
        if timestep < micro_count:
            received = passed_along(result, "section", 1)
    activations = lax.dynamic_slice_in_dim(jnp.stack(results), section_index, micro_count, 0)
    stored_all = jax.tree.map(lambda *pieces: jnp.stack(pieces), *stored_steps)
    received_grad = jnp.zeros_like(inputs[0])
    total = None
    shards = None
    grad_steps = []
    for timestep in range(micro_count + 1):
        micro_index = timestep - 1 + section_index
        in_range = (micro_index >= 0) & (micro_index < micro_count)
        clipped = jnp.clip(micro_index, 0, micro_count - 1)
        slot_index = jnp.clip(micro_index + section_index, 0, micro_count)
        stored = jax.tree.map(
            lambda stacked: lax.dynamic_index_in_dim(stacked, slot_index, 0, keepdims=False),
            stored_all,
        )
        segment_rows = lax.dynamic_index_in_dim(segments, clipped, 0, keepdims=False)
        same_segment = segment_rows[:, :, None] == segment_rows[:, None, :]
        grad_out = jnp.where(
            first_section, received_grad, cotangent[min(timestep, micro_count - 1)]
        )
        grad_in, gradients = layer_backward(grad_out, same_segment, weights, stored)
        gradients = tuple((jnp.where(in_range, member, 0.0) for member in gradients))
        grad_steps.append(grad_in)
        if timestep < micro_count:
            received_grad = passed_along(grad_in, "section", -1)
        total = add_tuples(total, gradients)
    packed = pack(total)
    shards = (
        lax.psum_scatter(packed[0], "dp", scatter_dimension=0, tiled=True),
        lax.psum_scatter(packed[1], "dp", scatter_dimension=0, tiled=True),
        lax.psum_scatter(packed[2], "dp", scatter_dimension=0, tiled=True),
        lax.psum_scatter(packed[3], "dp", scatter_dimension=0, tiled=True),
        lax.psum_scatter(packed[4], "dp", scatter_dimension=0, tiled=True),
        lax.psum_scatter(packed[5], "dp", scatter_dimension=0, tiled=True),
        lax.psum_scatter(packed[6], "dp", scatter_dimension=0, tiled=True),
    )
    gathered = (
        lax.all_gather(shards[0].astype(jnp.bfloat16), "dp", axis=0, tiled=True).astype(
            jnp.float32
        ),
        lax.all_gather(shards[1].astype(jnp.bfloat16), "dp", axis=0, tiled=True).astype(
            jnp.float32
        ),
        lax.all_gather(shards[2].astype(jnp.bfloat16), "dp", axis=0, tiled=True).astype(
            jnp.float32
        ),
        lax.all_gather(shards[3].astype(jnp.bfloat16), "dp", axis=0, tiled=True).astype(
            jnp.float32
        ),
        lax.all_gather(shards[4].astype(jnp.bfloat16), "dp", axis=0, tiled=True).astype(
            jnp.float32
        ),
        lax.all_gather(shards[5].astype(jnp.bfloat16), "dp", axis=0, tiled=True).astype(
            jnp.float32
        ),
        lax.all_gather(shards[6].astype(jnp.bfloat16), "dp", axis=0, tiled=True).astype(
            jnp.float32
        ),
    )
    input_gradients = lax.dynamic_slice_in_dim(
        jnp.stack(grad_steps), 1 - section_index, micro_count, 0
    )
    outputs = unpack(gathered, query_weight.shape[1], inner_weight.shape[2])
    return (
        activations[None],
        input_gradients[None],
        outputs[0],
        outputs[1],
        outputs[2],
        outputs[3],
        outputs[4],
        outputs[5],
        outputs[6],
        outputs[7],
        outputs[8],
        outputs[9],
        outputs[10],
        outputs[11],
        outputs[12],
        outputs[13],
        outputs[14],
    )


def solution(mesh):
    placed = (
        P(None, "dp", None, None),
        P(None, "dp", None),
        P(None, "dp", None, None),
        P("section", None, None),
        P("section", None),
        P("section", None, None),
        P("section", None, None),
        P("section", None),
        P("section", None, None),
        P("section", None),
        P("section", None),
        P("section", None),
        P("section", None, None),
        P("section", None),
        P("section", None, None),
        P("section", None),
        P("section", None),
        P("section", None),
    )
    return jax.shard_map(
        body,
        mesh=mesh,
        in_specs=placed,
        out_specs=(
            P("section", None, "dp", None, None),
            P("section", None, "dp", None, None),
            P("section", None, None),
            P("section", None),
            P("section", None, None),
            P("section", None, None),
            P("section", None),
            P("section", None, None),
            P("section", None),
            P("section", None),
            P("section", None),
            P("section", None, None),
            P("section", None),
            P("section", None, None),
            P("section", None),
            P("section", None),
            P("section", None),
        ),
        check_vma=False,
    )
```

profile of v0, /device:TPU:0, one launch (start us, length us, event | category | flops | bytes accessed | tf_op | source)
XLA Modules:
  0.0 1477.4 jit_solution(12455504728727620754)
XLA Ops:
  37.4 20.1 %add_bitcast_fusion.3 = (f32[1,1,512,3072]{3,2,1,0:T(8,128)}, bf16[512,3072]{1,0:T(8,128)(2,1)S(1)}) fusion(f32[3072]{0:T(1024)S(1)} %bitcast.974, bf16[1,768,3072]{2,1,0:T(8,128)(2,1)} %param.30, f32[512,768]{1,0:T(8,128)S(1)} %get-tuple-element.110, f32[768]{0:T(1024)S(1)} %get-tuple-element.152, f32[768]{0:T(1024)S(1)} %get-tuple-element.153, ...), kind=kOutput, calls=%fused_computation.195 | convolution fusion | flops 2521694208 | bytes 15751168 | tf_op jit(solution)/shard_map/dot_general | solution.py:26
  61.9 5.8 collective-permute-start
  72.4 11.1 collective-permute-done
  101.2 4.0 fusion.211
  106.6 20.1 %add_bitcast_fusion.2 = (f32[1,1,512,3072]{3,2,1,0:T(8,128)}, bf16[512,3072]{1,0:T(8,128)(2,1)S(1)}) fusion(f32[3072]{0:T(1024)S(1)} %bitcast.975, bf16[1,768,3072]{2,1,0:T(8,128)(2,1)} %param.30, f32[768]{0:T(1024)S(1)} %get-tuple-element.152, f32[768]{0:T(1024)S(1)} %get-tuple-element.153, f32[512]{0:T(512)S(1)} %add_rsqrt_fusion.3, ...), kind=kOutput, calls=%fused_computation.194 | convolution fusion | flops 2521694208 | bytes 15751168 | tf_op jit(solution)/shard_map/dot_general | solution.py:26
  130.4 5.1 collective-permute-start.1
  138.7 12.6 collective-permute-done.1
  167.3 5.0 fusion.210
  173.7 20.4 %add_bitcast_fusion.1 = (f32[1,1,512,3072]{3,2,1,0:T(8,128)}, bf16[512,3072]{1,0:T(8,128)(2,1)S(1)}) fusion(f32[3072]{0:T(1024)S(1)} %bitcast.976, bf16[1,768,3072]{2,1,0:T(8,128)(2,1)} %param.30, f32[768]{0:T(1024)S(1)} %get-tuple-element.152, f32[768]{0:T(1024)S(1)} %get-tuple-element.153, f32[512]{0:T(512)S(1)} %add_rsqrt_fusion.1, ...), kind=kOutput, calls=%fused_computation.193 | convolution fusion | flops 2521694208 | bytes 15751168 | tf_op jit(solution)/shard_map/dot_general | solution.py:26
  200.3 6.3 fusion.293
  206.7 6.3 fusion.306
  223.9 6.4 pad_maximum_fusion
  230.3 20.3 %convert_reduce_fusion.2 = (f32[3072]{0:T(1024)}, bf16[512,3072]{1,0:T(8,128)(2,1)}) fusion(bf16[1,3072,768]{2,1,0:T(8,128)(2,1)} %param.32, bf16[1,512,1,1,1,1,768]{6,1,5,4,3,2,0:T(8,128)(2,1)S(1)} %fusion.176, f32[3,1,512,3072]{3,2,1,0:T(8,128)S(1)} %pad_maximum_fusion, s32[]{:T(128)S(6)} %min.31), kind=kOutput, calls=%fused_computation.93 | convolution fusion | flops 2532307968 | bytes 14954500 | tf_op jit(solution)/shard_map/rlf,df->rld/dot_general | solution.py:34
  250.7 7.5 multiply_reduce_fusion.5
  267.6 11.8 multiply_reduce_fusion.2
  281.0 7.2 multiply_convert_fusion.2
  293.3 4.8 convert_reduce_fusion.14
  298.1 7.6 fusion.278
  324.6 6.7 fusion.150
  339.1 20.5 %convert_reduce_fusion.1 = (f32[3072]{0:T(1024)}, bf16[512,3072]{1,0:T(8,128)(2,1)S(1)}) fusion(bf16[1,3072,768]{2,1,0:T(8,128)(2,1)S(1)} %bitcast.985, bf16[1,512,768]{2,1,0:T(8,128)(2,1)S(1)} %get-tuple-element.53, f32[3,1,512,3072]{3,2,1,0:T(8,128)} %copy-done.10, s32[]{:T(128)S(6)} %min.33), kind=kOutput, calls=%fused_computation.92 | convolution fusion | flops 2532307968 | bytes 14954500 | tf_op jit(solution)/shard_map/rlf,df->rld/dot_general | solution.py:34
  359.7 3.8 multiply_reduce_fusion.4
  373.0 13.6 multiply_reduce_fusion.1
  386.6 7.0 multiply_convert_fusion.1
  399.7 3.9 convert_reduce_fusion.13
  409.8 8.3 fusion.148
  423.4 6.4 fusion.249
  429.8 4.0 fusion.254
  433.9 5.2 fusion.251
  444.3 20.5 %convert_reduce_fusion = (f32[3072]{0:T(1024)}, bf16[512,3072]{1,0:T(8,128)(2,1)S(1)}) fusion(bf16[1,3072,768]{2,1,0:T(8,128)(2,1)S(1)} %bitcast.987, bf16[1,512,768]{2,1,0:T(8,128)(2,1)S(1)} %get-tuple-element.55, f32[3,1,512,3072]{3,2,1,0:T(8,128)} %copy-done.10, s32[]{:T(128)S(6)} %min.35), kind=kOutput, calls=%fused_computation.91 | convolution fusion | flops 2532307968 | bytes 14954500 | tf_op jit(solution)/shard_map/rlf,df->rld/dot_general | solution.py:34
  476.1 9.6 convert_reduce_fusion.12
  485.7 9.7 multiply_reduce_fusion
  495.4 7.2 multiply_convert_fusion
  502.5 4.0 multiply_convert_fusion.3
  530.7 4.2 select_add_fusion.3
  538.1 4.2 select_add_fusion.2
  545.7 4.4 select_add_fusion.1
  553.2 8.6 add_bitcast_fusion
  561.8 5.9 copy.149
  567.7 11.5 select_add_fusion
  579.3 10.8 reshape.3367
  590.1 582.8 %all-reduce.10 = (bf16[589824]{0:T(1024)(128)(2,1)}, bf16[9216]{0:T(1024)(128)(2,1)}, bf16[589824]{0:T(1024)(128)(2,1)}, bf16[589824]{0:T(1024)(128)(2,1)}, bf16...) all-reduce(f32[589824]{0:T(1024)} %reshape.3353, ...), channel_id=2, replica_groups=mesh['section'=2,'dp'=16] {'dp'}, use_global_device_ids=true, to_apply=%region_45.46.clone | all-reduce | flops 7087104 | bytes 42522624
  1190.4 70.3 %all-reduce = bf16[9216]{0:T(1024)(128)(2,1)} all-reduce(bf16[9216]{0:T(1024)(128)(2,1)} %dynamic-update-slice), channel_id=1, replica_groups=mesh['section'=2,'dp'=16] {'dp'}, use_global_device_ids=true, to_apply=%add | all-reduce | flops 9216 | bytes 36864
  1283.9 27.8 %all-gather.11.cloned.1.call-done = bf16[589824]{0:T(1024)(128)(2,1)} async-done(((bf16[36864]{0:T(1024)(128)(2,1)}), bf16[589824]{0:T(1024)(128)(2,1)}) %all-gather.11.cloned.1.call-update) | async-done | bytes 1179664 | tf_op jit(solution)/shard_map/all_gather | solution.py:355
  1315.0 36.1 %all-gather.13.cloned.1.call-done = bf16[589824]{0:T(1024)(128)(2,1)} async-done(((bf16[36864]{0:T(1024)(128)(2,1)}), bf16[589824]{0:T(1024)(128)(2,1)}) %all-gather.13.cloned.1.call-update) | async-done | bytes 1179664 | tf_op jit(solution)/shard_map/all_gather | solution.py:358
  1354.5 51.8 %all-gather.15.cloned.1.call-done = bf16[2359296]{0:T(1024)(128)(2,1)} async-done(((bf16[147456]{0:T(1024)(128)(2,1)}), bf16[2359296]{0:T(1024)(128)(2,1)}) %all-gather.15.cloned.1.call-update) | async-done | bytes 4718608 | tf_op jit(solution)/shard_map/all_gather | solution.py:361
  1406.2 8.8 reshape.3383
  1415.0 45.4 %all-gather.17.cloned.1.call-done = bf16[2359296]{0:T(1024)(128)(2,1)} async-done(((bf16[147456]{0:T(1024)(128)(2,1)}), bf16[2359296]{0:T(1024)(128)(2,1)}) %all-gather.17.cloned.1.call-update) | async-done | bytes 4718608 | tf_op jit(solution)/shard_map/all_gather | solution.py:364
  1460.3 10.0 reshape.3384
  (719 shorter events, 262.5 us)
Async XLA Ops:
  7.2 28.8 %copy-start = (bf16[1,768,768]{2,1,0:T(8,128)(2,1)S(1)}, bf16[1,768,768]{2,1,0:T(8,128)(2,1)}, u32[]{:S(2)}) copy-start(bf16[1,768,768]{2,1,0:T(8,128)(2,1)} %param.26) | copy-start | bytes 3538948
  7.2 1270.0 %all-gather.7.cloned.1.call-start = ((), (), s32[]{:S(2)}) async-start(), calls=%async_computation | async-start | bytes 1253376 | tf_op jit(solution)/shard_map/all_gather | solution.py:349
  8.1 49.4 %copy-start.183 = (f32[768]{0:T(1024)}, f32[768]{0:T(1024)S(1)}, u32[]{:S(2)}) copy-start(f32[768]{0:T(1024)S(1)} %convert_reduce_fusion.20) | copy-start | bytes 9220
  10.1 25.9 %copy-start.186 = (f32[768]{0:T(1024)}, f32[768]{0:T(1024)S(1)}, u32[]{:S(2)}) copy-start(f32[768]{0:T(1024)S(1)} %convert_reduce_fusion.23) | copy-start | bytes 9220
  12.0 24.0 %copy-start.72 = (bf16[1,1,512,768]{3,2,1,0:T(8,128)(2,1)}, bf16[1,1,512,768]{3,2,1,0:T(8,128)(2,1)S(1)}, u32[]{:S(2)}) copy-start(bf16[1,1,512,768]{3,2,1,0:T(8,128)(2,1)S(1)} %slice_select_fusion.1) | copy-start | bytes 2359300
  35.9 21.5 %copy-start.101 = (bf16[12,64,512]{2,1,0:T(8,128)(2,1)}, bf16[12,64,512]{2,1,0:T(8,128)(2,1)S(1)}, u32[]{:S(2)}) copy-start(bf16[12,64,512]{2,1,0:T(8,128)(2,1)S(1)} %fusion.212) | copy-start | bytes 2359300
  36.0 21.5 %slice-start.19 = ((s8[4718592]{0:T(1024)(128)(4,1)}), s8[4194304]{0:T(1024)(128)(4,1)S(1)}, s32[]{:S(2)}) async-start(s8[4718592]{0:T(1024)(128)(4,1)} %bitcast.978), calls=%async_computation.25 | async-start | bytes 8388608
  60.5 24.3 %copy-start.33 = (bf16[1,768,768]{2,1,0:T(8,128)(2,1)S(1)}, bf16[1,768,768]{2,1,0:T(8,128)(2,1)}, u32[]{:S(2)}) copy-start(bf16[1,768,768]{2,1,0:T(8,128)(2,1)} %param.24) | copy-start | bytes 3538948
  60.9 69.1 %copy-start.120 = (f32[768]{0:T(1024)}, f32[768]{0:T(1024)S(1)}, u32[]{:S(2)}) copy-start(f32[768]{0:T(1024)S(1)} %get-tuple-element.154) | copy-start | bytes 9220
  60.9 380.7 %copy-start.112 = (f32[768]{0:T(1024)}, f32[768]{0:T(1024)S(1)}, u32[]{:S(2)}) copy-start(f32[768]{0:T(1024)S(1)} %get-tuple-element.155) | copy-start | bytes 9220
  61.9 21.6 %collective-permute-start = (bf16[1,512,768]{2,1,0:T(8,128)(2,1)S(1)}, bf16[1,512,768]{2,1,0:T(8,128)(2,1)}, u32[]{:S(2)}, u32[]{:S(2)}) collective-permute-start(bf16[1,512,768]{2,1,0:T(8,128)(2,1)S(1)} %fusion.491), channel_id=1, source_target_pairs={{0,16},{1,17},{2,18},{3,19},{4,20},{5,21},{6,22},{7,23},{8,24},{9,... | collective-permute-start | bytes 2359304 | tf_op jit(solution)/shard_map/ppermute | solution.py:15
  105.2 21.4 %copy-start.103 = (bf16[12,64,512]{2,1,0:T(8,128)(2,1)}, bf16[12,64,512]{2,1,0:T(8,128)(2,1)S(1)}, u32[]{:S(2)}) copy-start(bf16[12,64,512]{2,1,0:T(8,128)(2,1)S(1)} %fusion.211) | copy-start | bytes 2359300
  105.3 21.4 %slice-start.21 = ((s8[4718592]{0:T(1024)(128)(4,1)}), s8[4194304]{0:T(1024)(128)(4,1)S(1)}, s32[]{:S(2)}) async-start(s8[4718592]{0:T(1024)(128)(4,1)} %bitcast.980), calls=%async_computation.27 | async-start | bytes 8388608
  129.6 83.4 %copy-start.6 = (f32[1,512,768]{2,1,0:T(8,128)}, f32[1,512,768]{2,1,0:T(8,128)S(1)}, u32[]{:S(2)}) copy-start(f32[1,512,768]{2,1,0:T(8,128)S(1)} %get-tuple-element.118) | copy-start | bytes 4718596
  129.7 21.7 %copy-start.54 = (bf16[2,1,512,768]{3,2,1,0:T(8,128)(2,1)S(1)}, bf16[2,1,512,768]{3,2,1,0:T(8,128)(2,1)}, u32[]{:S(2)}) copy-start(bf16[2,1,512,768]{3,2,1,0:T(8,128)(2,1)} %param.18) | copy-start | bytes 4718596
  129.7 21.8 %copy-start.34 = (bf16[1,768,768]{2,1,0:T(8,128)(2,1)S(1)}, bf16[1,768,768]{2,1,0:T(8,128)(2,1)}, u32[]{:S(2)}) copy-start(bf16[1,768,768]{2,1,0:T(8,128)(2,1)} %param.24) | copy-start | bytes 3538948
  129.7 21.8 %copy-start.190 = (f32[768]{0:T(1024)S(1)}, f32[768]{0:T(1024)}, u32[]{:S(2)}) copy-start(f32[768]{0:T(1024)} %copy-done.189) | copy-start | bytes 9220
  129.7 21.6 %copy-start.135 = (f32[512]{0:T(512)}, f32[512]{0:T(512)S(1)}, u32[]{:S(2)}) copy-start(f32[512]{0:T(512)S(1)} %broadcast_multiply_fusion.8) | copy-start | bytes 6148
  130.0 21.3 %copy-start.147 = (f32[512]{0:T(512)}, f32[512]{0:T(512)S(1)}, u32[]{:S(2)}) copy-start(f32[512]{0:T(512)S(1)} %add_rsqrt_fusion.2) | copy-start | bytes 6148
  130.4 21.9 %copy-start.192 = (f32[768]{0:T(1024)S(1)}, f32[768]{0:T(1024)}, u32[]{:S(2)}) copy-start(f32[768]{0:T(1024)} %copy-done.191) | copy-start | bytes 9220
  130.4 21.9 %copy-start.205 = (bf16[1,768,768]{2,1,0:T(8,128)(2,1)S(1)}, bf16[1,768,768]{2,1,0:T(8,128)(2,1)}, u32[]{:S(2)}) copy-start(bf16[1,768,768]{2,1,0:T(8,128)(2,1)} %param.21) | copy-start | bytes 3538948
  130.4 20.9 %collective-permute-start.1 = (bf16[1,512,768]{2,1,0:T(8,128)(2,1)S(1)}, bf16[1,512,768]{2,1,0:T(8,128)(2,1)S(1)}, u32[]{:S(2)}, u32[]{:S(2)}) collective-permute-start(bf16[1,512,768]{2,1,0:T(8,128)(2,1)S(1)} %add_convert_fusion.5), channel_id=1, source_target_pairs={{0,16},{1,17},{2,18},{3,19},{4,20},{5,21},{6,22},{7,23},{8,24},{9,... | collective-permute-start | bytes 2359304 | tf_op jit(solution)/shard_map/ppermute | solution.py:15
  172.3 21.8 %copy-start.105 = (bf16[12,64,512]{2,1,0:T(8,128)(2,1)}, bf16[12,64,512]{2,1,0:T(8,128)(2,1)S(1)}, u32[]{:S(2)}) copy-start(bf16[12,64,512]{2,1,0:T(8,128)(2,1)S(1)} %fusion.210) | copy-start | bytes 2359300
  172.4 21.8 %slice-start.23 = ((s8[4718592]{0:T(1024)(128)(4,1)}), s8[4194304]{0:T(1024)(128)(4,1)S(1)}, s32[]{:S(2)}) async-start(s8[4718592]{0:T(1024)(128)(4,1)} %bitcast.982), calls=%async_computation.29 | async-start | bytes 8388608
  173.3 41.5 %copy-start.21 = (f32[1,512,768]{2,1,0:T(8,128)}, f32[1,512,768]{2,1,0:T(8,128)S(1)}, u32[]{:S(2)}) copy-start(f32[1,512,768]{2,1,0:T(8,128)S(1)} %get-tuple-element.122) | copy-start | bytes 4718596
  173.3 20.8 %copy-start.161 = (f32[512]{0:T(512)}, f32[512]{0:T(512)S(1)}, u32[]{:S(2)}) copy-start(f32[512]{0:T(512)S(1)} %broadcast_multiply_fusion.7) | copy-start | bytes 6148
  213.3 37.3 %copy-start.1 = (f32[3,1,512,768]{3,2,1,0:T(8,128)}, f32[3,1,512,768]{3,2,1,0:T(8,128)S(1)}, u32[]{:S(2)}) copy-start(f32[3,1,512,768]{3,2,1,0:T(8,128)S(1)} %pad_maximum_fusion.2) | copy-start | bytes 14155780
  217.3 40.9 %copy-start.2 = (f32[3,1,512,768]{3,2,1,0:T(8,128)}, f32[3,1,512,768]{3,2,1,0:T(8,128)S(1)}, u32[]{:S(2)}) copy-start(f32[3,1,512,768]{3,2,1,0:T(8,128)S(1)} %pad_maximum_fusion.3) | copy-start | bytes 14155780
  223.3 27.3 %copy-start.156 = (f32[512]{0:T(512)}, f32[512]{0:T(512)S(1)}, u32[]{:S(2)}) copy-start(f32[512]{0:T(512)S(1)} %negate_multiply_fusion.11) | copy-start | bytes 6148
  313.1 46.5 %copy-start.174 = (f32[512]{0:T(512)}, f32[512]{0:T(512)S(1)}, u32[]{:S(2)}) copy-start(f32[512]{0:T(512)S(1)} %broadcast_multiply_fusion) | copy-start | bytes 6148
  316.5 19.8 %collective-permute-start.2 = (bf16[1,512,768]{2,1,0:T(8,128)(2,1)S(1)}, bf16[1,512,768]{2,1,0:T(8,128)(2,1)S(1)}, u32[]{:S(2)}, u32[]{:S(2)}) collective-permute-start(bf16[1,512,768]{2,1,0:T(8,128)(2,1)S(1)} %bitcast.949), channel_id=1, source_target_pairs={{16,0},{17,1},{18,2},{19,3},{20,4},{21,5},{22,6},{23,7},{24,8},{25... | collective-permute-start | bytes 2359304 | tf_op jit(solution)/shard_map/ppermute | solution.py:15
  337.6 22.0 %slice-start.13 = ((s8[4718592]{0:T(1024)(128)(4,1)}), s8[4194304]{0:T(1024)(128)(4,1)S(1)}, s32[]{:S(2)}) async-start(s8[4718592]{0:T(1024)(128)(4,1)} %bitcast.899), calls=%async_computation.19 | async-start | bytes 8388608
  337.6 22.0 %slice-start.29 = ((s8[4718592]{0:T(1024)(128)(4,1)}), s8[4194304]{0:T(1024)(128)(4,1)S(1)}, s32[]{:S(2)}) async-start(s8[4718592]{0:T(1024)(128)(4,1)} %bitcast.988), calls=%async_computation.35 | async-start | bytes 8388608
  339.1 20.6 %copy-start.166 = (f32[512]{0:T(512)S(1)}, f32[512]{0:T(512)}, u32[]{:S(2)}) copy-start(f32[512]{0:T(512)} %copy-done.165) | copy-start | bytes 6148
  421.5 18.7 %collective-permute-start.3 = (bf16[1,512,768]{2,1,0:T(8,128)(2,1)S(1)}, bf16[1,512,768]{2,1,0:T(8,128)(2,1)S(1)}, u32[]{:S(2)}, u32[]{:S(2)}) collective-permute-start(bf16[1,512,768]{2,1,0:T(8,128)(2,1)S(1)} %fusion.184), channel_id=1, source_target_pairs={{16,0},{17,1},{18,2},{19,3},{20,4},{21,5},{22,6},{23,7},{24,8},{25... | collective-permute-start | bytes 2359304 | tf_op jit(solution)/shard_map/ppermute | solution.py:15
  423.4 20.8 %slice-start.27 = ((s8[4718592]{0:T(1024)(128)(4,1)}), s8[4194304]{0:T(1024)(128)(4,1)S(1)}, s32[]{:S(2)}) async-start(s8[4718592]{0:T(1024)(128)(4,1)} %bitcast.986), calls=%async_computation.33 | async-start | bytes 8388608
  441.7 23.1 %slice-start.15 = ((s8[4718592]{0:T(1024)(128)(4,1)}), s8[4194304]{0:T(1024)(128)(4,1)S(1)}, s32[]{:S(2)}) async-start(s8[4718592]{0:T(1024)(128)(4,1)} %bitcast.901), calls=%async_computation.21 | async-start | bytes 8388608
  441.7 23.1 %slice-start.31 = ((s8[4718592]{0:T(1024)(128)(4,1)}), s8[4194304]{0:T(1024)(128)(4,1)S(1)}, s32[]{:S(2)}) async-start(s8[4718592]{0:T(1024)(128)(4,1)} %bitcast.990), calls=%async_computation.37 | async-start | bytes 8388608
  590.0 594.7 %copy-start.5 = (f32[512,768]{1,0:T(8,128)S(1)}, f32[512,768]{1,0:T(8,128)}, u32[]{:S(2)}) copy-start(f32[512,768]{1,0:T(8,128)} %copy-done.3) | copy-start | bytes 4718596
  590.0 594.7 %copy-start.113 = (f32[768]{0:T(1024)S(1)}, f32[768]{0:T(1024)}, u32[]{:S(2)}) copy-start(f32[768]{0:T(1024)} %copy-done.112) | copy-start | bytes 9220
  590.0 594.7 %copy-start.122 = (f32[768]{0:T(1024)S(1)}, f32[768]{0:T(1024)}, u32[]{:S(2)}) copy-start(f32[768]{0:T(1024)} %copy-done.120) | copy-start | bytes 9220
  590.0 594.7 %copy-start.134 = (f32[512]{0:T(512)S(1)}, f32[512]{0:T(512)}, u32[]{:S(2)}) copy-start(f32[512]{0:T(512)} %copy-done.133) | copy-start | bytes 6148
  1174.4 106.1 %all-gather.9.cloned.1.call-start = ((), (), s32[]{:S(2)}) async-start(), calls=%async_computation.1 | async-start | bytes 1253376 | tf_op jit(solution)/shard_map/all_gather | solution.py:352
  1176.0 135.7 %all-gather.11.cloned.1.call-start = ((), (), s32[]{:S(2)}) async-start(), calls=%async_computation.2 | async-start | bytes 1253376 | tf_op jit(solution)/shard_map/all_gather | solution.py:355
  1177.6 173.5 %all-gather.13.cloned.1.call-start = ((), (), s32[]{:S(2)}) async-start(), calls=%async_computation.3 | async-start | bytes 1253376 | tf_op jit(solution)/shard_map/all_gather | solution.py:358
  1179.2 227.0 %all-gather.15.cloned.1.call-start = ((), (), s32[]{:S(2)}) async-start(), calls=%async_computation.4 | async-start | bytes 5013504 | tf_op jit(solution)/shard_map/all_gather | solution.py:361
  1181.7 278.7 %all-gather.17.cloned.1.call-start = ((), (), s32[]{:S(2)}) async-start(), calls=%async_computation.5 | async-start | bytes 5013504 | tf_op jit(solution)/shard_map/all_gather | solution.py:364
  1185.8 87.4 %copy-start.65 = (bf16[12,64,512]{2,1,0:T(8,128)(2,1)S(1)}, bf16[12,64,512]{2,1,0:T(8,128)(2,1)}, u32[]{:S(2)}) copy-start(bf16[12,64,512]{2,1,0:T(8,128)(2,1)} %copy-done.64) | copy-start | bytes 2359300
  (204 other events, 1575.4 us)
Sparse Core Ops, SparseCore 0:
  1174.5 57.1 all-gather.6
  1234.6 37.3 all-gather.8
  1274.2 37.3 all-gather.10
  1313.8 37.2 all-gather.12
  1353.8 52.3 all-gather.14
  1408.4 51.9 all-gather.16
where the time goes:
time: 1490 us; the launch traced here: 1480 us
  blocking collectives  653 us (44%)
  matrix products  378 us (25%)
  waiting for transfers between devices  189 us (13%)
  local copies, waits for them, and re-layouts  122 us (8%)
  other arithmetic  101 us (7%)
  between operations  20.1 us (1%)
    unnamed x2, blocking collectives  653 us
    dot_general x18, matrix products, back_dot(): jnp.einsum('rlf,df->rld', grad_in, weight, preferred_element_type=jnp.flo...  91.1 us
    dot_general x18, matrix products, matmul(): return jnp.dot(left, right, preferred_element_type=jnp.float32)  89.7 us
    dot_general x18, matrix products, weight_grad(): jnp.einsum('rld,rlf->df', left, right, preferred_element_type=jnp.float32)  81.4 us
    all_gather x1, waiting for transfers between devices, body(): lax.all_gather(shards[4].astype(jnp.bfloat16), 'dp', axis=0, tiled=True)  51.8 us
    all_gather x1, waiting for transfers between devices, body(): lax.all_gather(shards[5].astype(jnp.bfloat16), 'dp', axis=0, tiled=True)  45.4 us
    unnamed x497, local copies, waits for them, and re-layouts  40.2 us
    all_gather x1, waiting for transfers between devices, body(): lax.all_gather(shards[3].astype(jnp.bfloat16), 'dp', axis=0, tiled=True)  36.1 us
  transfers between devices with their start and end apart: 10, of which 8 were waited for; matrix products, arithmetic and copies ran while one was open for 6% of the time, Pallas kernels for 0%

commit v1 on v0

v1 whole, which is shorter than its diff:
```python
from functools import partial

import jax
import jax.numpy as jnp
from jax import lax
from jax.experimental import pallas as pl
from jax.experimental.pallas import tpu as pltpu
from jax.sharding import PartitionSpec as P

HEADS = 12
HEAD = 64
LANES = 128
TILE = 256
VMEM_LIMIT = 60 * 1024 * 1024
BF = jnp.bfloat16
F32 = jnp.float32
ANY = pl.BlockSpec(memory_space=pl.ANY)
SMEM = pl.BlockSpec(memory_space=pltpu.SMEM)
VMEM = pl.BlockSpec(memory_space=pltpu.VMEM)


def dot(left, right):
    return lax.dot_general(left, right, (((1,), (0,)), ((), ())), preferred_element_type=F32)


def dot_nt(left, right):
    return lax.dot_general(left, right, (((1,), (1,)), ((), ())), preferred_element_type=F32)


def dot_tn(left, right):
    return lax.dot_general(left, right, (((0,), (0,)), ((), ())), preferred_element_type=F32)


def gelu_pair(u):
    z = jnp.abs(u) * 0.7071067811865476
    d = 1.0 + 0.3275911 * z
    t = pl.reciprocal(d, approx=True)
    t = t * (2.0 - d * t)
    poly = t * (0.127414796 + t * (-0.142248368 + t * (0.7107068705 + t * (-0.7265760135 + t * 0.5307027145))))
    bell = jnp.exp(-0.5 * u * u)
    tail = poly * bell
    cdf = jnp.where(u >= 0, 1.0 - tail, tail)
    return u * cdf, cdf + u * (bell * 0.3989422804014327)


def ds(index, size):
    return pl.ds(pl.multiple_of(index * size, size), size)


def forward_kernel(go, seg_row, bq, bv, bo, ga, sa, bi, bu, gf, sf,
                   x_h, wq_h, wk_h, wv_h, wo_h, wi_h, wu_h, *rest, n_alias, micro):
    rest = rest[n_alias:]
    outs, scratch = rest[:15], rest[15:]
    (res_h, x_o, q_h, k_h, v_h, e_h, inv_h, ctx_h, na_h, ra_h, hid_h, der_h, act_h, nf_h, rf_h) = outs
    (x, wq, wk, wv, wo, wi, wu, q, k, v, va, e, inv, ctx, na, ra, hid, der, act, nf, rf, res, mask, work, hidden, sin, sout) = scratch
    rows, width = x.shape
    wide = wi.shape[1]

    @pl.when(go[0] == 1)
    def _():
        loads = [(x_h if micro is None else x_h.at[micro], x), (wq_h, wq), (wk_h, wk), (wv_h, wv), (wo_h, wo), (wi_h, wi), (wu_h, wu)]
        loads = [pltpu.make_async_copy(a, b, sin.at[i]) for i, (a, b) in enumerate(loads)]
        for c in loads:
            c.start()
        stores = {}

        def put(i, src, dst):
            c = pltpu.make_async_copy(src, dst, sout.at[i])
            c.start()
            stores[i] = c

        ids = jnp.broadcast_to(seg_row[...].astype(F32), (8, rows))
        mask[...] = jnp.where(jnp.transpose(ids)[:, 0:1] == ids[0:1, :], 0.0, -1e30)
        loads[0].wait()
        put(0, x, x_o)
        loads[1].wait()
        nt = width // TILE
        for j in range(nt):
            cols = slice(j * TILE, (j + 1) * TILE)
            q[:, cols] = ((dot(x[...], wq[:, cols]) + bq[:, cols].astype(F32)).astype(BF) * HEAD ** -0.5).astype(BF)
        put(1, q, q_h)
        loads[2].wait()
        for j in range(nt):
            cols = slice(j * TILE, (j + 1) * TILE)
            k[:, cols] = dot(x[...], wk[:, cols]).astype(BF)
        put(2, k, k_h)
        loads[3].wait()
        for j in range(nt):
            cols = slice(j * TILE, (j + 1) * TILE)
            vv = (dot(x[...], wv[:, cols]) + bv[:, cols].astype(F32)).astype(BF)
            v[:, cols] = vv
            one = jnp.ones((rows, LANES), BF)
            for h in range(TILE // LANES):
                at = (j * (TILE // LANES) + h) * TILE
                va[:, at:at + LANES] = vv[:, h * LANES:(h + 1) * LANES]
                va[:, at + LANES:at + TILE] = one
        put(3, v, v_h)

        low = lax.broadcasted_iota(jnp.int32, (1, LANES), 1) < HEAD
        qb = 128

        def pair(p, _):
            kp = k[:, ds(p, LANES)]
            vp = va[:, ds(p, TILE)]
            kz = [jnp.where(low, kp, jnp.zeros_like(kp)), jnp.where(low, jnp.zeros_like(kp), kp)]
            for b in range(rows // qb):
                rr = slice(b * qb, (b + 1) * qb)
                qp = q[rr, ds(p, LANES)]
                parts = []
                for h in range(2):
                    s = dot_nt(qp, kz[h]) + mask[rr, :]
                    top = jnp.max(s, axis=-1, keepdims=True)
                    ee = jnp.exp(s - top).astype(BF)
                    e[2 * p + h, rr, :] = ee
                    o = dot(ee, vp)
                    r = 1.0 / o[:, LANES:]
                    parts.append((o[:, :LANES] * r, r))
                inv[rr, ds(p, LANES)] = jnp.where(low, parts[0][1], parts[1][1])
                ctx[rr, ds(p, LANES)] = jnp.where(low, parts[0][0], parts[1][0]).astype(BF)
            return 0

        lax.fori_loop(0, width // LANES, pair, 0)
        put(4, e, e_h)
        put(5, inv, inv_h)
        put(6, ctx, ctx_h)
        loads[4].wait()
        for j in range(nt):
            cols = slice(j * TILE, (j + 1) * TILE)
            work[:, cols] = dot(ctx[...], wo[:, cols]) + bo[:, cols].astype(F32) + x[:, cols].astype(F32)

        def norm(b, _):
            rr = ds(b, 64)
            t = work[rr, :]
            t = t - jnp.mean(t, axis=-1, keepdims=True)
            r = lax.rsqrt(jnp.mean(t * t, axis=-1, keepdims=True) + 1e-12)
            n = t * r
            h = n * ga[...].astype(F32) + sa[...].astype(F32)
            na[rr, :] = n.astype(BF)
            ra[rr, :] = jnp.broadcast_to(r, (64, LANES))
            hidden[rr, :] = h
            hid[rr, :] = h.astype(BF)
            return 0

        lax.fori_loop(0, rows // 64, norm, 0, unroll=2)
        put(7, na, na_h)
        put(8, ra, ra_h)
        put(9, hid, hid_h)
        loads[5].wait()

        def feed(j, _):
            cols = ds(j, TILE)
            u = dot(hid[...], wi[:, cols]) + bi[:, cols].astype(F32)
            a, g = gelu_pair(u)
            act[:, cols] = a.astype(BF)
            der[:, cols] = g.astype(BF)
            return 0

        lax.fori_loop(0, wide // TILE, feed, 0, unroll=2)
        put(10, der, der_h)
        put(11, act, act_h)
        loads[6].wait()
        for j in range(nt):
            cols = slice(j * TILE, (j + 1) * TILE)
            work[:, cols] = dot(act[...], wu[:, cols]) + bu[:, cols].astype(F32) + hidden[:, cols]

        def last(b, _):
            rr = ds(b, 64)
            t = work[rr, :]
            t = t - jnp.mean(t, axis=-1, keepdims=True)
            r = lax.rsqrt(jnp.mean(t * t, axis=-1, keepdims=True) + 1e-12)
            n = t * r
            nf[rr, :] = n.astype(BF)
            rf[rr, :] = jnp.broadcast_to(r, (64, LANES))
            res[rr, :] = (n * gf[...].astype(F32) + sf[...].astype(F32)).astype(BF)
            return 0

        lax.fori_loop(0, rows // 64, last, 0, unroll=2)
        put(12, res, res_h)
        put(13, nf, nf_h)
        put(14, rf, rf_h)
        for c in stores.values():
            c.wait()


def run_forward(go, seg, x, w, micro=None, saved=None):
    rows, width = x.shape[-2:]
    wide = w["wi"].shape[1]
    sd = jax.ShapeDtypeStruct
    act = sd((rows, width), BF)
    out_shape = [act] * 5 + [sd((HEADS, rows, rows), BF), sd((rows, width), F32), act, act, sd((rows, LANES), F32), act,
                             sd((rows, wide), BF), sd((rows, wide), BF), act, sd((rows, LANES), F32)]
    vm = pltpu.VMEM
    scratch = [vm((rows, width), BF)] + [vm((width, width), BF)] * 4 + [vm((width, wide), BF), vm((wide, width), BF)]
    scratch += [vm((rows, width), BF)] * 3 + [vm((rows, 2 * width), BF), vm((HEADS, rows, rows), BF), vm((rows, width), F32)]
    scratch += [vm((rows, width), BF)] * 2 + [vm((rows, LANES), F32), vm((rows, width), BF)] + [vm((rows, wide), BF)] * 2
    scratch += [vm((rows, width), BF), vm((rows, LANES), F32), vm((rows, width), BF), vm((rows, rows), F32)]
    scratch += [vm((rows, width), F32)] * 2
    scratch += [pltpu.SemaphoreType.DMA((7,)), pltpu.SemaphoreType.DMA((15,))]
    alias = () if saved is None else tuple(saved)
    args = [go, seg, w["bq"], w["bv"], w["bo"], w["ga"], w["sa"], w["bi"], w["bu"], w["gf"], w["sf"],
            x, w["wq"], w["wk"], w["wv"], w["wo"], w["wi"], w["wu"], *alias]
    outs = pl.pallas_call(
        partial(forward_kernel, n_alias=len(alias), micro=micro),
        out_shape=out_shape,
        in_specs=[SMEM] + [VMEM] * 10 + [ANY] * (7 + len(alias)),
        out_specs=[ANY] * 15,
        scratch_shapes=scratch,
        input_output_aliases={18 + i: 1 + i for i in range(len(alias))},
        compiler_params=pltpu.CompilerParams(vmem_limit_bytes=VMEM_LIMIT),
        cost_estimate=pl.CostEstimate(flops=2 * rows * 10 * width * width, bytes_accessed=40_000_000, transcendentals=0),
        name="forward",
    )(*args)
    return outs[0], outs[1:]


def feed_back_kernel(go, gf, g_h, nf_h, rf_h, der_h, wu_h, wi_h, *rest, n_alias, micro):
    rest = rest[n_alias:]
    og_h, ig_h, hg_h, small_h = rest[:4]
    g, nf, rf, der, wu, wi, og, ig, hg, small, sin, sout = rest[4:]
    rows, width = g.shape
    wide = der.shape[1]

    @pl.when(go[0] == 1)
    def _():
        loads = [(g_h if micro is None else g_h.at[micro], g), (nf_h, nf), (rf_h, rf), (wu_h, wu), (der_h, der), (wi_h, wi)]
        loads = [pltpu.make_async_copy(a, b, sin.at[i]) for i, (a, b) in enumerate(loads)]
        for c in loads:
            c.start()
        for c in loads[:3]:
            c.wait()

        def norm(b, sums):
            rr = ds(b, 64)
            t = g[rr, :].astype(F32)
            n = nf[rr, :].astype(F32)
            s = t * gf[...].astype(F32)
            m1 = jnp.mean(s, axis=-1, keepdims=True)
            m2 = jnp.mean(s * n, axis=-1, keepdims=True)
            f = (s - m1 - n * m2) * rf[rr, 0:1]
            hg[rr, :] = f
            low = f.astype(BF)
            og[rr, :] = low
            parts = (t * n, t, low.astype(F32))
            return tuple(a + jnp.sum(b.reshape(8, 8, width), axis=0) for a, b in zip(sums, parts))

        zero = jnp.zeros((8, width), F32)
        sums = lax.fori_loop(0, rows // 64, norm, (zero, zero, zero), unroll=2)
        small[...] = jnp.zeros_like(small)
        for i in range(3):
            small[i:i + 1, :width] = jnp.sum(sums[i], axis=0, keepdims=True)
        c0 = pltpu.make_async_copy(og, og_h, sout.at[0])
        c0.start()
        loads[3].wait()
        loads[4].wait()

        def inner(j, _):
            cols = ds(j, TILE)
            t = dot_nt(og[...], wu[cols, :]) * der[:, cols].astype(F32)
            low = t.astype(BF)
            ig[:, cols] = low
            small[3:4, cols] = jnp.sum(low.astype(F32), axis=0, keepdims=True)
            return 0

        lax.fori_loop(0, wide // TILE, inner, 0, unroll=2)
        c1 = pltpu.make_async_copy(ig, ig_h, sout.at[1])
        c1.start()
        loads[5].wait()
        for j in range(width // TILE):
            cols = slice(j * TILE, (j + 1) * TILE)
            hg[:, cols] = hg[:, cols] + dot_nt(ig[...], wi[cols, :])
        c2 = pltpu.make_async_copy(hg, hg_h, sout.at[2])
        c2.start()
        c3 = pltpu.make_async_copy(small, small_h, sout.at[3])
        c3.start()
        c0.wait()
        c1.wait()
        c2.wait()
        c3.wait()


def run_feed_back(go, g, saved, w, micro=None, old=None):
    (x, q, k, v, e, inv, ctx, na, ra, hid, der, act, nf, rf) = saved
    rows, width = g.shape[-2:]
    wide = der.shape[1]
    sd, vm = jax.ShapeDtypeStruct, pltpu.VMEM
    alias = () if old is None else tuple(old)
    outs = pl.pallas_call(
        partial(feed_back_kernel, n_alias=len(alias), micro=micro),
        out_shape=[sd((rows, width), BF), sd((rows, wide), BF), sd((rows, width), F32), sd((8, wide), F32)],
        in_specs=[SMEM, VMEM] + [ANY] * (6 + len(alias)),
        out_specs=[ANY] * 4,
        scratch_shapes=[vm((rows, width), BF), vm((rows, width), BF), vm((rows, LANES), F32), vm((rows, wide), BF),
                        vm((wide, width), BF), vm((width, wide), BF), vm((rows, width), BF), vm((rows, wide), BF), vm((rows, width), F32),
                        vm((8, wide), F32), pltpu.SemaphoreType.DMA((6,)), pltpu.SemaphoreType.DMA((4,))],
        input_output_aliases={8 + i: i for i in range(len(alias))},
        compiler_params=pltpu.CompilerParams(vmem_limit_bytes=VMEM_LIMIT),
        cost_estimate=pl.CostEstimate(flops=4 * rows * wide * width, bytes_accessed=20_000_000, transcendentals=0),
        name="feed_back",
    )(go, w["gf"], g, nf, rf, der, w["wu"], w["wi"], *alias)
    return outs


def attention_back_kernel(go, ga, hg_h, na_h, ra_h, wo_h, inv_h, ctx_h, q_h, k_h, v_h, e_h, wq_h, wk_h, wv_h, *rest, n_alias):
    rest = rest[n_alias:]
    lg_h, bg_h, dq_h, dk_h, dv_h, small_h = rest[:6]
    (hg, na, ra, wo, inv, ctx, q, k, v, e, wq, wk, wv, bg, cg, dq, dk, dv, lg, small, sin, sout) = rest[6:]
    rows, width = bg.shape

    @pl.when(go[0] == 1)
    def _():
        loads = [(hg_h, hg), (na_h, na), (ra_h, ra), (wo_h, wo), (inv_h, inv), (ctx_h, ctx), (q_h, q), (k_h, k), (v_h, v),
                 (e_h, e), (wq_h, wq), (wk_h, wk), (wv_h, wv)]
        loads = [pltpu.make_async_copy(a, b, sin.at[i]) for i, (a, b) in enumerate(loads)]
        for c in loads:
            c.start()
        for c in loads[:3]:
            c.wait()

        def norm(b, sums):
            rr = ds(b, 64)
            t = hg[rr, :]
            n = na[rr, :].astype(F32)
            s = t * ga[...].astype(F32)
            m1 = jnp.mean(s, axis=-1, keepdims=True)
            m2 = jnp.mean(s * n, axis=-1, keepdims=True)
            f = (s - m1 - n * m2) * ra[rr, 0:1]
            hg[rr, :] = f
            low = f.astype(BF)
            bg[rr, :] = low
            parts = (t * n, t, low.astype(F32))
            return tuple(a + jnp.sum(b.reshape(8, 8, width), axis=0) for a, b in zip(sums, parts))

        zero = jnp.zeros((8, width), F32)
        sums = lax.fori_loop(0, rows // 64, norm, (zero, zero, zero), unroll=2)
        small[...] = jnp.zeros_like(small)
        for i in range(3):
            small[i:i + 1, :] = jnp.sum(sums[i], axis=0, keepdims=True)
        puts = []

        def put(src, dst):
            c = pltpu.make_async_copy(src, dst, sout.at[len(puts)])
            c.start()
            puts.append(c)

        put(bg, bg_h)
        loads[3].wait()
        for j in range(width // TILE):
            cols = slice(j * TILE, (j + 1) * TILE)
            cg[:, cols] = dot_nt(bg[...], wo[cols, :]).astype(BF)
        for c in loads[4:10]:
            c.wait()

        low = lax.broadcasted_iota(jnp.int32, (1, LANES), 1) < HEAD

        def pair(p, _):
            cols = ds(p, LANES)
            kp = k[:, cols]
            vp = v[:, cols]
            qp = q[:, cols]
            cp = cg[:, cols].astype(F32)
            prod = cp * ctx[:, cols].astype(F32)
            ip = inv[:, cols]
            co = (cp * ip).astype(BF)
            zb = jnp.zeros_like(kp)
            dqs, dks, dvs = [], [], []
            for h in range(2):
                mine = low if h == 0 else jnp.logical_not(low)
                weighted = jnp.sum(jnp.where(mine, prod * ip, 0.0), axis=-1, keepdims=True)
                ch = jnp.where(mine, co, zb)
                ee = e[2 * p + h]
                dp = dot_nt(ch, vp) - weighted
                sg = (ee.astype(F32) * dp).astype(BF)
                dvs.append(dot_tn(ee, ch))
                dqs.append(dot(sg, jnp.where(mine, kp, zb)))
                dks.append(dot_tn(sg, jnp.where(mine, qp, zb)))
            dq[:, cols] = ((dqs[0] + dqs[1]) * HEAD ** -0.5).astype(BF)
            dk[:, cols] = (dks[0] + dks[1]).astype(BF)
            dv[:, cols] = (dvs[0] + dvs[1]).astype(BF)
            return 0

        lax.fori_loop(0, width // LANES, pair, 0)
        put(dq, dq_h)
        put(dk, dk_h)
        put(dv, dv_h)
        for c in loads[10:]:
            c.wait()
        for j in range(width // TILE):
            cols = slice(j * TILE, (j + 1) * TILE)
            t = hg[:, cols] + dot_nt(dq[...], wq[cols, :]) + dot_nt(dk[...], wk[cols, :]) + dot_nt(dv[...], wv[cols, :])
            lg[:, cols] = t.astype(BF)
        put(lg, lg_h)
        small[3:4, :] = jnp.sum(dq[...].astype(F32), axis=0, keepdims=True)
        small[4:5, :] = jnp.sum(dv[...].astype(F32), axis=0, keepdims=True)
        put(small, small_h)
        for c in puts:
            c.wait()


def run_attention_back(go, hg, saved, w, old=None):
    (x, q, k, v, e, inv, ctx, na, ra, hid, der, act, nf, rf) = saved
    rows, width = x.shape
    sd, vm = jax.ShapeDtypeStruct, pltpu.VMEM
    alias = () if old is None else tuple(old)
    row = vm((rows, width), BF)
    sq = vm((width, width), BF)
    outs = pl.pallas_call(
        partial(attention_back_kernel, n_alias=len(alias)),
        out_shape=[sd((rows, width), BF)] * 5 + [sd((8, width), F32)],
        in_specs=[SMEM, VMEM] + [ANY] * (13 + len(alias)),
        out_specs=[ANY] * 6,
        scratch_shapes=[vm((rows, width), F32), row, vm((rows, LANES), F32), sq, vm((rows, width), F32), row, row, row, row,
                        vm((HEADS, rows, rows), BF), sq, sq, sq, row, row, row, row, row, row,
                        vm((8, width), F32), pltpu.SemaphoreType.DMA((13,)), pltpu.SemaphoreType.DMA((6,))],
        input_output_aliases={15 + i: 1 + i for i in range(len(alias))},
        compiler_params=pltpu.CompilerParams(vmem_limit_bytes=VMEM_LIMIT),
        cost_estimate=pl.CostEstimate(flops=16 * rows * width * width, bytes_accessed=30_000_000, transcendentals=0),
        name="attention_back",
    )(go, w["ga"], hg, na, ra, w["wo"], inv, ctx, q, k, v, e, w["wq"], w["wk"], w["wv"], *alias)
    return outs[0], outs[1:]


def wgrad_kernel(half, a0, a1, g0, g1, o):
    o[0] = (dot_tn(a0[...], g0[...]) + dot_tn(a1[...], g1[...])).astype(BF)


def run_wgrad(half, a, g, block, split_left):
    rows, m = a[0].shape
    n = g[0].shape[1]
    if split_left:
        gi, aj, ha, hg, gn = 1, m // 2 // block, m // 2 // block, 0, n
    else:
        gn = m
        gi, aj, ha, hg = n // 2 // gn, m // block, 0, n // 2 // gn
    sa = pl.BlockSpec((rows, block), lambda i, j, h: (0, h[0] * ha + j))
    sg = pl.BlockSpec((rows, gn), lambda i, j, h: (0, h[0] * hg + i))
    return pl.pallas_call(
        wgrad_kernel,
        grid_spec=pltpu.PrefetchScalarGridSpec(
            num_scalar_prefetch=1, grid=(gi, aj), in_specs=[sa, sa, sg, sg],
            out_specs=pl.BlockSpec((1, block, gn), lambda i, j, h: (i * aj + j, 0, 0))),
        out_shape=jax.ShapeDtypeStruct((gi * aj, block, gn), BF),
        compiler_params=pltpu.CompilerParams(vmem_limit_bytes=VMEM_LIMIT),
        cost_estimate=pl.CostEstimate(flops=2 * rows * m * n, bytes_accessed=2 * (2 * rows * (m + n) + m * n), transcendentals=0),
        name="weight_gradient",
    )(half, a[0], a[1], g[0], g[1])


def attention_wgrad_kernel(half, fs0, fs1, as0, as1, *rest):
    ctx, x, bg, dq, dk, dv = [rest[2 * i:2 * i + 2] for i in range(6)]
    o, a_s, g_s, sems = rest[12:]
    width = a_s.shape[-1]
    chunk = o.shape[1] - 16
    sides = (((ctx, bg), (x, dq)), ((x, dk), (x, dv)))
    for side in range(2):
        @pl.when(half[0] == side)
        def _(side=side):
            for s in range(2):
                for m in range(2):
                    pltpu.make_async_copy(sides[side][s][0][m], a_s.at[s, m], sems.at[0, s, m]).start()
                    pltpu.make_async_copy(sides[side][s][1][m], g_s.at[s, m], sems.at[1, s, m]).start()
    o[:, chunk:, :] = jnp.zeros((o.shape[0], 16, width), BF)
    fs = fs0[...] + fs1[...]
    at = as0[...] + as1[...]
    lines = [at[3:4], at[4:5], at[2:3], at[0:1], at[1:2], fs[2:3, :width], fs[0:1, :width], fs[1:2, :width]]
    lines += [fs[3:4, i * width:(i + 1) * width] for i in range(fs.shape[1] // width)]
    lines += [jnp.zeros((16 - len(lines), width), F32)]
    o[0, chunk:, :] = jnp.concatenate(lines, axis=0).astype(BF)
    for s in range(2):
        for m in range(2):
            pltpu.make_async_copy(dv[0], a_s.at[s, m], sems.at[0, s, m]).wait()
            pltpu.make_async_copy(dv[0], g_s.at[s, m], sems.at[1, s, m]).wait()
        per = width // chunk
        for t in range(per):
            cols = slice(t * chunk, (t + 1) * chunk)
            r = dot_tn(a_s[s, 0, :, cols], g_s[s, 0]) + dot_tn(a_s[s, 1, :, cols], g_s[s, 1])
            o[s * per + t, :chunk, :] = r.astype(BF)


def run_attention_wgrad(half, feed_small, att_small, ctx, x, bg, dq, dk, dv):
    rows, width = ctx[0].shape
    chunk = 2 * width // 8
    args = [a for pair in (ctx, x, bg, dq, dk, dv) for a in pair]
    return pl.pallas_call(
        attention_wgrad_kernel,
        out_shape=jax.ShapeDtypeStruct((8, chunk + 16, width), BF),
        in_specs=[SMEM] + [VMEM] * 4 + [ANY] * 12,
        out_specs=VMEM,
        scratch_shapes=[pltpu.VMEM((2, 2, rows, width), BF), pltpu.VMEM((2, 2, rows, width), BF), pltpu.SemaphoreType.DMA((2, 2, 2))],
        compiler_params=pltpu.CompilerParams(vmem_limit_bytes=VMEM_LIMIT),
        cost_estimate=pl.CostEstimate(flops=8 * rows * width * width, bytes_accessed=9_000_000, transcendentals=0),
        name="attention_weight_gradient",
    )(half, *feed_small, *att_small, *args)


def unpack_kernel(place, *rest, kind, extra):
    mine, other = rest[:8], rest[8]
    n_out = {"rows": 1, "columns": 1, "four": 4}[kind]
    outs = rest[9:9 + n_out]
    small = rest[9 + n_out:-4]
    low, high, sin, sout = rest[-4:]
    total, width = low.shape[1:]
    chunk = total - extra
    loads = [pltpu.make_async_copy(mine[u], low.at[u], sin.at[u]) for u in range(8)]
    loads += [pltpu.make_async_copy(other.at[u], low.at[8 + u], sin.at[8 + u]) for u in range(8)]
    for c in loads:
        c.start()
    for u in range(16):
        core = place[0] if u < 8 else 1 - place[0]
        rank = place[1] if u < 8 else 7 - place[1]
        index = core * 8 + lax.rem(rank + 9 - u % 8, 8)
        loads[u].wait()
        high[u] = low[u, :chunk, :].astype(F32)
        if kind == "rows":
            pltpu.make_async_copy(high.at[u], outs[0].at[pl.ds(pl.multiple_of(index * chunk, 8), chunk), :], sout.at[u]).start()
        else:
            per = width // chunk
            block, row = index // per, lax.rem(index, per)
            where = pl.ds(pl.multiple_of(row * chunk, 8), chunk)
            if kind == "columns":
                cols = pl.ds(pl.multiple_of(block * width, width), width)
                pltpu.make_async_copy(high.at[u], outs[0].at[where, cols], sout.at[u]).start()
            else:
                for n in range(4):
                    @pl.when(block == n)
                    def _(n=n, u=u, where=where):
                        pltpu.make_async_copy(high.at[u], outs[n].at[where, :], sout.at[u]).start()
    if extra:
        u = lax.rem(place[1] + 1, 8)
        t = low[u, chunk:, :].astype(F32)
        for i in range(8):
            small[i][...] = t[i:i + 1]
        for i in range(small[8].shape[1] // width):
            small[8][:, i * width:(i + 1) * width] = t[8 + i:9 + i]
    for u in range(16):
        pltpu.make_async_copy(high.at[u], outs[0].at[:chunk, :width], sout.at[u]).wait()


def run_unpack(place, pieces, other, kind, wide=0):
    total, width = pieces[0].shape
    extra = 16 if kind == "four" else 0
    chunk = total - extra
    sd = jax.ShapeDtypeStruct
    if kind == "rows":
        shapes = [sd((16 * chunk, width), F32)]
    elif kind == "columns":
        shapes = [sd((width, 16 * chunk), F32)]
    else:
        shapes = [sd((4 * chunk, width), F32)] * 4
    small = [sd((1, width), F32)] * 8 + [sd((1, wide), F32)] if extra else []
    return pl.pallas_call(
        partial(unpack_kernel, kind=kind, extra=extra),
        out_shape=shapes + small,
        in_specs=[SMEM] + [ANY] * 9,
        out_specs=[ANY] * len(shapes) + [VMEM] * len(small),
        scratch_shapes=[pltpu.VMEM((16, total, width), BF), pltpu.VMEM((16, chunk, width), F32),
                        pltpu.SemaphoreType.DMA((16,)), pltpu.SemaphoreType.DMA((16,))],
        compiler_params=pltpu.CompilerParams(vmem_limit_bytes=VMEM_LIMIT),
        cost_estimate=pl.CostEstimate(flops=0, bytes_accessed=6 * 16 * total * width, transcendentals=0),
        name="unpack",
    )(place, *pieces, other)


def ring_tables():
    chips = [(z, 0) for z in range(4)] + [(z, 1) for z in reversed(range(4))]
    step = []
    for at, (z, y) in enumerate(chips):
        for core in range(2):
            nz, ny = chips[(at + 1) % 8] if core == 0 else chips[at - 1]
            step.append((z * 4 + y * 2 + core, nz * 4 + ny * 2 + core))
    swap = [(d, d ^ 1) for d in range(16)]
    return step, swap


def ring_place():
    d = lax.axis_index("dp")
    z, y, core = d // 4, (d // 2) % 2, d % 2
    at = jnp.where(y == 0, z, 7 - z)
    return core, jnp.where(core == 0, at, 7 - at)


def after(value, *earlier):
    return lax.optimization_barrier((value, *earlier))[0]


def ring_sum(keep, got, rank, step):
    def own(index):
        index = lax.rem(index, 8)
        return lax.dynamic_index_in_dim(keep, index, 0, keepdims=False) + lax.dynamic_index_in_dim(got, index, 0, keepdims=False)

    current = own(rank)
    for s in range(7):
        current = lax.ppermute(current, "dp", step) + own(rank + 7 - s)
    pieces = [current]
    for s in range(7):
        current = lax.ppermute(current, "dp", step)
        pieces.append(current)
    return pieces


def body(inputs, segments, cotangent, query_weight, query_bias, key_weight, value_weight, value_bias, output_weight, output_bias,
         attention_gain, attention_shift, inner_weight, inner_bias, outer_weight, outer_bias, feed_gain, feed_shift):
    micros, local, rows, width = inputs.shape
    wide = inner_weight.shape[2]
    w = dict(wq=query_weight[0], wk=key_weight[0], wv=value_weight[0], wo=output_weight[0], wi=inner_weight[0], wu=outer_weight[0],
             bq=query_bias, bv=value_bias, bo=output_bias, ga=attention_gain, sa=attention_shift, bi=inner_bias, bu=outer_bias,
             gf=feed_gain, sf=feed_shift)
    x_all = inputs.reshape(micros, rows, width)
    g_all = cotangent.reshape(micros, rows, width)
    section = lax.axis_index("section")
    first = section == 0
    on0 = jnp.reshape(1 - section, (1,)).astype(jnp.int32)
    on1 = jnp.reshape(section, (1,)).astype(jnp.int32)
    up = partial(lax.ppermute, axis_name="section", perm=[(0, 1)])
    down = partial(lax.ppermute, axis_name="section", perm=[(1, 0)])

    r00, s0 = run_forward(on0, segments[0], x_all, w, micro=0)
    x10 = up(r00)
    r01, s1 = run_forward(after(on0, r00), segments[1], x_all, w, micro=1)
    x11 = up(r01)
    r10, s0 = run_forward(after(on1, r01), segments[0], x10, w, saved=s0)
    f0 = run_feed_back(on1, g_all, s0, w, micro=0)
    l10, a0 = run_attention_back(on1, f0[2], s0, w)
    g00 = down(l10)
    r11, s1 = run_forward(after(on1, l10), segments[1], x11, w, saved=s1)
    f0 = run_feed_back(after(on0, r11), g00, s0, w, old=f0)
    l00, a0 = run_attention_back(on0, f0[2], s0, w, old=a0)
    f1 = run_feed_back(after(on1, l00), g_all, s1, w, micro=1)
    l11, a1 = run_attention_back(on1, f1[2], s1, w)
    g01 = down(l11)
    f1 = run_feed_back(on0, g01, s1, w, old=f1)
    (x0, q0, k0, v0, e0, inv0, ctx0, na0, ra0, hid0, der0, act0, nf0, rf0) = s0
    (x1, q1, k1, v1, e1, inv1, ctx1, na1, ra1, hid1, der1, act1, nf1, rf1) = s1
    core, rank = ring_place()
    there = jnp.reshape(1 - core, (1,)).astype(jnp.int32)
    here = jnp.reshape(core, (1,)).astype(jnp.int32)
    place = jnp.stack([core, rank]).astype(jnp.int32)
    step, swap = ring_tables()

    def outer(h):
        return run_wgrad(h, (act0, act1), (f0[0], f1[0]), 256, True)

    def inner(h):
        return run_wgrad(h, (hid0, hid1), (f0[1], f1[1]), 256, False)

    def rest(h):
        return run_attention_wgrad(h, (f0[3], f1[3]), (a0[4], a1[4]), (ctx0, ctx1), (x0, x1), (a0[0], a1[0]), (a0[1], a1[1]),
                                   (a0[2], a1[2]), (a0[3], a1[3]))

    def reduced(make):
        sent = make(there)
        got = lax.ppermute(sent, "dp", swap)
        keep = make(after(here, sent))
        shape = (8, -1, width)
        pieces = ring_sum(keep.reshape(shape), got.reshape(shape), rank, step)
        other = lax.ppermute(jnp.stack(pieces), "dp", swap)
        return pieces, other

    ring = lax.axis_size("dp") == 16
    if ring:
        p1, o1 = reduced(outer)
        p2, o2 = reduced(inner)
        l01, a1 = run_attention_back(on0, f1[2], s1, w, old=a1)
        p3, o3 = reduced(rest)
        (outer_g,) = run_unpack(place, p1, o1, "rows")
        (inner_g,) = run_unpack(place, p2, o2, "columns")
        fours = run_unpack(place, p3, o3, "four", wide)
    else:
        zero, one = jnp.zeros((1,), jnp.int32), jnp.ones((1,), jnp.int32)
        l01, a1 = run_attention_back(on0, f1[2], s1, w, old=a1)
        sums = [lax.psum(jnp.stack([make(zero).reshape(8, -1, width), make(one).reshape(8, -1, width)]), "dp").astype(F32)
                for make in (outer, inner, rest)]
        outer_g = sums[0].reshape(wide, width)
        inner_g = sums[1].reshape(wide // width, width, width).transpose(1, 0, 2).reshape(width, wide)
        tail = 2 * width // 8
        lines = sums[2][0, 0, tail:]
        fours = list(sums[2][:, :, :tail].reshape(4, width, width)) + [lines[i:i + 1] for i in range(8)]
        fours.append(lines[8:8 + wide // width].reshape(1, wide))
    (wo_g, wq_g, wk_g, wv_g, bq_g, bv_g, bo_g, ga_g, sa_g, bu_g, gf_g, sf_g, bi_g) = fours
    activations = jnp.where(first, jnp.stack([r00, r01]), jnp.stack([r10, r11]))
    input_gradients = jnp.where(first, jnp.stack([l00, l01]), jnp.stack([l10, l11]))
    shape = (1, micros, local, rows, width)
    return (activations.reshape(shape), input_gradients.reshape(shape), wq_g[None], bq_g, wk_g[None], wv_g[None], bv_g, wo_g[None], bo_g,
            ga_g, sa_g, inner_g[None], bi_g, outer_g[None], bu_g, gf_g, sf_g)


def solution(mesh):
    rows3 = P(None, "dp", None, None)
    matrix, vector = P("section", None, None), P("section", None)
    results = P("section", None, "dp", None, None)
    return jax.shard_map(
        body,
        mesh=mesh,
        in_specs=(rows3, P(None, "dp", None), rows3, matrix, vector, matrix, matrix, vector, matrix, vector, vector, vector,
                  matrix, vector, matrix, vector, vector, vector),
        out_specs=(results, results, matrix, vector, matrix, matrix, vector, matrix, vector, vector, vector, matrix, vector,
                   matrix, vector, vector, vector),
        check_vma=False,
    )
```

time: 1490 us -> 455 us (0.31)
  blocking collectives: 653 us -> 0 us
  matrix products: 378 us -> 0 us
  Pallas kernels: 0 us -> 194 us
  local copies, waits for them, and re-layouts: 122 us -> 24.2 us
  other arithmetic: 101 us -> 27.7 us
  waiting for transfers between devices: 189 us -> 127 us
  starting transfers between devices: 14.6 us -> 73.1 us
  between operations: 20.1 us -> 1.56 us
    unnamed x2 -> x0, blocking collectives: 653 us -> none
    dot_general x75 -> x0, matrix products: 378 us -> none  [the longest x18 91.1 us: back_dot(): jnp.einsum('rlf,df->rld', grad_in, weight, preferred_element_type=jnp.flo...]
    pallas_call x0 -> x21, Pallas kernels: none -> 194 us  [the longest x4 57.9 us: run_forward(): pl.pallas_call(partial(forward_kernel, n_alias=len(alias), micro=micro),...]
    all_gather x6 -> x0, waiting for transfers between devices: 161 us -> none  [the longest x1 51.8 us: body(): lax.all_gather(shards[4].astype(jnp.bfloat16), 'dp', axis=0, tiled=True)]
    ppermute x4 -> x52, waiting for transfers between devices: 28.2 us -> 127 us  [the longest x1 50.9 us: body(): g00 = down(l10)]
    ppermute x4 -> x52, starting transfers between devices: 14.3 us -> 73.1 us  [the longest x21 33.4 us: ring_sum(): current = lax.ppermute(current, 'dp', step) + own(rank + 7 - s)]
    reduce_sum x28 -> x0, other arithmetic: 31.3 us -> none  [the longest x3 10.8 us: layer_forward(): total = jnp.sum(expo, axis=-1, keepdims=True)]
    another operation x6 -> x3, local copies, waits for them, and re-layouts: 32.1 us -> 2.34 us  [reduced(): other = lax.ppermute(jnp.stack(pieces), 'dp', swap)]
  transfers between devices with their start and end apart: 10 -> 52, of which waited for: 8 -> 39; matrix products, arithmetic and copies ran while one was open for 6% -> 10% of each run, Pallas kernels for 0% -> 24%
where the time goes in v1:
time: 455 us; the launch traced here: 448 us
  Pallas kernels  194 us (43%)
  waiting for transfers between devices  127 us (28%)
  starting transfers between devices  73.1 us (16%)
  other arithmetic  27.7 us (6%)
  local copies, waits for them, and re-layouts  24.2 us (5%)
    pallas_call x4, Pallas kernels, run_forward(): pl.pallas_call(partial(forward_kernel, n_alias=len(alias), micro=micro),...  57.9 us
    ppermute x1, waiting for transfers between devices, body(): g00 = down(l10)  50.9 us
    pallas_call x4, Pallas kernels, run_attention_back(): pl.pallas_call(partial(attention_back_kernel, n_alias=len(alias)), out_sh...  47 us
    ppermute x21, starting transfers between devices, ring_sum(): current = lax.ppermute(current, 'dp', step) + own(rank + 7 - s)  33.4 us
    ppermute x21, starting transfers between devices, ring_sum(): current = lax.ppermute(current, 'dp', step)  33.3 us
    pallas_call x4, Pallas kernels, run_wgrad(): pl.pallas_call(wgrad_kernel, grid_spec=pltpu.PrefetchScalarGridSpec(num_s...  30 us
    ppermute x1, waiting for transfers between devices, body(): g01 = down(l11)  28.5 us
    pallas_call x4, Pallas kernels, run_feed_back(): pl.pallas_call(partial(feed_back_kernel, n_alias=len(alias), micro=micro)...  27.3 us
  transfers between devices with their start and end apart: 52, of which 39 were waited for; matrix products, arithmetic and copies ran while one was open for 10% of the time, Pallas kernels for 24%

profile of v1, /device:TPU:0, one launch (start us, length us, event | category | flops | bytes accessed | tf_op | source)
XLA Modules:
  0.0 447.6 jit_solution(3292325557404853264)
XLA Ops:
  1.9 27.5 %forward.4 = (bf16[512,768]{1,0:T(8,128)(2,1)}, bf16[512,768]{1,0:T(8,128)(2,1)}, bf16[512,768]{1,0:T(8,128)(2,1)}, bf16[512,768]{1,0:T(8,128)(2,1)}, bf16[512,7...) custom-call(s32[1]{0:T(128)} %bitcast.go, ...), custom_call_target="tpu_custom_call" | custom-call | flops 6039797760 | bytes 40000000 | tf_op jit(solution)/shard_map/forward/pallas_call | solution.py:202
  30.8 28.1 %forward.5 = (bf16[512,768]{1,0:T(8,128)(2,1)}, bf16[512,768]{1,0:T(8,128)(2,1)}, bf16[512,768]{1,0:T(8,128)(2,1)}, bf16[512,768]{1,0:T(8,128)(2,1)}, bf16[512,7...) custom-call(s32[1]{0:T(128)} %bitcast.go, ...), custom_call_target="tpu_custom_call" | custom-call | flops 6039797760 | bytes 40000000 | tf_op jit(solution)/shard_map/forward/pallas_call | solution.py:202
  63.2 7.1 %attention_back.4 = (bf16[512,768]{1,0:T(8,128)(2,1)}, bf16[512,768]{1,0:T(8,128)(2,1)}, bf16[512,768]{1,0:T(8,128)(2,1)}, bf16[512,768]{1,0:T(8,128)(2,1)}, bf16[512,768]{1,0:T(8,128)(2,1)}, /*index=5*/f32[8,768]{1,0:T(8,128)}) custom-call(s32[1]{0:T(128)} %bitcast.12.go, bf16[1,768]{1,0:T(2,128)(2,1)} %ga.15, f32[512,768]{1,0:T(8,128)} %get-tuple-element.160.hg_h.rest_2_, ...), custom_call_target="tpu_custom_call" | custom-call | flops 4831838208 | bytes 30000000 | tf_op jit(solution)/shard_map/attention_back/pallas_call | solution.py:406
  71.6 6.7 %collective-permute-done.1.x_h = bf16[512,768]{1,0:T(8,128)(2,1)S(1)} collective-permute-done((bf16[512,768]{1,0:T(8,128)(2,1)}, bf16[512,768]{1,0:T(8,128)(2,1)S(1)}, u32[]{:S(2)}, u32[]{:S(2)}) %collective-permute-start.1) | collective-permute-done | bytes 786464 | tf_op jit(solution)/shard_map/ppermute | solution.py:619
  80.2 50.9 %collective-permute-done.2.g_h = bf16[512,768]{1,0:T(8,128)(2,1)S(1)} collective-permute-done((bf16[512,768]{1,0:T(8,128)(2,1)}, bf16[512,768]{1,0:T(8,128)(2,1)S(1)}, u32[]{:S(2)}, u32[]{:S(2)}) %collective-permute-start.2) | collective-permute-done | bytes 786464 | tf_op jit(solution)/shard_map/ppermute | solution.py:623
  132.0 13.1 %feed_back.5 = (bf16[512,768]{1,0:T(8,128)(2,1)}, bf16[512,3072]{1,0:T(8,128)(2,1)}, f32[512,768]{1,0:T(8,128)}, f32[8,3072]{1,0:T(8,128)}) custom-call(s32[1]{0:T(128)} %bitcast.go, bf16[1,768]{1,0:T(2,128)(2,1)} %gf.15, bf16[512,768]{1,0:T(8,128)(2,1)} %copy-done.30, ...), custom_call_target="tpu_custom_call", output_to_operand_aliasing={{0}: (8, {}), {1}: (9, {}), {2}: (10, {}), {3}: (11, {})} | custom-call | flops 4831838208 | bytes 20000000 | tf_op jit(solution)/shard_map/feed_back/pallas_call | solution.py:287
  145.0 19.3 %attention_back.5 = (bf16[512,768]{1,0:T(8,128)(2,1)}, bf16[512,768]{1,0:T(8,128)(2,1)}, bf16[512,768]{1,0:T(8,128)(2,1)}, bf16[512,768]{1,0:T(8,128)(2,1)}, bf16[512,768]{1,0:T(8,128)(2,1)}, /*index=5*/f32[8,768]{1,0:T(8,128)}) custom-call(s32[1]{0:T(128)} %bitcast.go, ...), custom_call_target="tpu_custom_call", output_to_operand_aliasing={{1}: (15, {}), {2}: (16, {}), {3}: (17, {}), {4}: (18, {}),... | custom-call | flops 4831838208 | bytes 30000000 | tf_op jit(solution)/shard_map/attention_back/pallas_call | solution.py:406
  167.5 28.5 %collective-permute-done.3.g_h = bf16[512,768]{1,0:T(8,128)(2,1)S(1)} collective-permute-done((bf16[512,768]{1,0:T(8,128)(2,1)}, bf16[512,768]{1,0:T(8,128)(2,1)S(1)}, u32[]{:S(2)}, u32[]{:S(2)}) %collective-permute-start.3) | collective-permute-done | bytes 786464 | tf_op jit(solution)/shard_map/ppermute | solution.py:629
  196.8 12.7 %feed_back.7 = (bf16[512,768]{1,0:T(8,128)(2,1)}, bf16[512,3072]{1,0:T(8,128)(2,1)}, f32[512,768]{1,0:T(8,128)}, f32[8,3072]{1,0:T(8,128)}) custom-call(s32[1]{0:T(128)} %bitcast.go, bf16[1,768]{1,0:T(2,128)(2,1)} %gf.15, bf16[512,768]{1,0:T(8,128)(2,1)} %copy-done.31, ...), custom_call_target="tpu_custom_call", output_to_operand_aliasing={{0}: (8, {}), {1}: (9, {}), {2}: (10, {}), {3}: (11, {})} | custom-call | flops 4831838208 | bytes 20000000 | tf_op jit(solution)/shard_map/feed_back/pallas_call | solution.py:287
  209.5 7.2 %weight_gradient.6 = bf16[6,256,768]{2,1,0:T(8,128)(2,1)} custom-call(s32[1]{0:T(128)} %bitcast.22.half, bf16[512,3072]{1,0:T(8,128)(2,1)} %get-tuple-element.251.a0, bf16[512,3072]{1,0:T(8,128)(2,1)} %get-tuple-element.252.a1, bf16[512,768]{1,0:T(8,128)(2,1)} %get-tuple-element.253.g0, bf16[512,768]{1,0:T(8,128)(2,1)} %get-tuple-element.254.g1), custom_call_target="tpu_custom_call" | custom-call | flops 2415919104 | bytes 12582912 | tf_op jit(solution)/shard_map/weight_gradient/pallas_call | solution.py:436
  216.8 7.7 %weight_gradient.4 = bf16[6,256,768]{2,1,0:T(8,128)(2,1)} custom-call(s32[1]{0:T(128)} %bitcast.22.half, bf16[512,768]{1,0:T(8,128)(2,1)} %get-tuple-element.245.a0, bf16[512,768]{1,0:T(8,128)(2,1)} %get-tuple-element.246.a1, bf16[512,3072]{1,0:T(8,128)(2,1)} %get-tuple-element.247.g0, bf16[512,3072]{1,0:T(8,128)(2,1)} %get-tuple-element.248.g1), custom_call_target="tpu_custom_call" | custom-call | flops 2415919104 | bytes 12582912 | tf_op jit(solution)/shard_map/weight_gradient/pallas_call | solution.py:436
  225.0 19.5 %attention_back.7 = (bf16[512,768]{1,0:T(8,128)(2,1)}, bf16[512,768]{1,0:T(8,128)(2,1)}, bf16[512,768]{1,0:T(8,128)(2,1)}, bf16[512,768]{1,0:T(8,128)(2,1)}, bf16[512,768]{1,0:T(8,128)(2,1)}, /*index=5*/f32[8,768]{1,0:T(8,128)}) custom-call(s32[1]{0:T(128)} %bitcast.go, ...), custom_call_target="tpu_custom_call", output_to_operand_aliasing={{1}: (15, {}), {2}: (16, {}), {3}: (17, {}), {4}: (18, {}),... | custom-call | flops 4831838208 | bytes 30000000 | tf_op jit(solution)/shard_map/attention_back/pallas_call | solution.py:406
  244.5 7.4 %attention_weight_gradient.2 = bf16[8,208,768]{2,1,0:T(8,128)(2,1)} custom-call(s32[1]{0:T(128)} %bitcast.22.half, f32[8,3072]{1,0:T(8,128)} %get-tuple-element.221.fs0, f32[8,3072]{1,0:T(8,128)} %get-tuple-element.222.fs1, f32[8,768]{1,0:T(8,128)} %get-tuple-element.223.as0, f32[8,768]{1,0:T(8,128)} %get-tuple-element.224.as1, ...), custom_call_target="tpu_custom_call" | custom-call | flops 2415919104 | bytes 9000000 | tf_op jit(solution)/shard_map/attention_weight_gradient/pallas_call | solution.py:483
  252.2 7.2 %weight_gradient.7 = bf16[6,256,768]{2,1,0:T(8,128)(2,1)} custom-call(s32[1]{0:T(128)} %bitcast.20.half, bf16[512,3072]{1,0:T(8,128)(2,1)} %get-tuple-element.251.a0, bf16[512,3072]{1,0:T(8,128)(2,1)} %get-tuple-element.252.a1, bf16[512,768]{1,0:T(8,128)(2,1)} %get-tuple-element.253.g0, bf16[512,768]{1,0:T(8,128)(2,1)} %get-tuple-element.254.g1), custom_call_target="tpu_custom_call" | custom-call | flops 2415919104 | bytes 12582912 | tf_op jit(solution)/shard_map/weight_gradient/pallas_call | solution.py:436
  259.4 7.7 %weight_gradient.5 = bf16[6,256,768]{2,1,0:T(8,128)(2,1)} custom-call(s32[1]{0:T(128)} %bitcast.20.half, bf16[512,768]{1,0:T(8,128)(2,1)} %get-tuple-element.245.a0, bf16[512,768]{1,0:T(8,128)(2,1)} %get-tuple-element.246.a1, bf16[512,3072]{1,0:T(8,128)(2,1)} %get-tuple-element.247.g0, bf16[512,3072]{1,0:T(8,128)(2,1)} %get-tuple-element.248.g1), custom_call_target="tpu_custom_call" | custom-call | flops 2415919104 | bytes 12582912 | tf_op jit(solution)/shard_map/weight_gradient/pallas_call | solution.py:436
  268.2 1.9 collective-permute-start.37
  272.5 1.6 collective-permute-start.21
  274.1 7.4 %attention_weight_gradient.3 = bf16[8,208,768]{2,1,0:T(8,128)(2,1)} custom-call(s32[1]{0:T(128)} %bitcast.20.half, f32[8,3072]{1,0:T(8,128)} %get-tuple-element.221.fs0, f32[8,3072]{1,0:T(8,128)} %get-tuple-element.222.fs1, f32[8,768]{1,0:T(8,128)} %get-tuple-element.223.as0, f32[8,768]{1,0:T(8,128)} %get-tuple-element.224.as1, ...), custom_call_target="tpu_custom_call" | custom-call | flops 2415919104 | bytes 9000000 | tf_op jit(solution)/shard_map/attention_weight_gradient/pallas_call | solution.py:483
  282.9 1.6 collective-permute-start.38
  290.7 1.6 collective-permute-start.39
  293.8 1.6 collective-permute-start.23
  297.3 1.6 collective-permute-start.6
  300.4 1.6 collective-permute-start.40
  302.6 1.6 collective-permute-start.24
  304.2 1.7 collective-permute-done.6
  307.0 1.7 collective-permute-start.7
  310.1 1.6 collective-permute-start.41
  312.3 1.6 collective-permute-start.25
  313.9 1.7 collective-permute-done.7
  316.7 1.6 collective-permute-start.8
  319.9 1.6 collective-permute-start.42
  322.1 1.6 collective-permute-start.26
  323.7 1.7 collective-permute-done.8
  326.5 1.7 collective-permute-start.9
  329.6 1.6 collective-permute-start.43
  331.8 1.6 collective-permute-start.27
  333.4 1.7 collective-permute-done.9
  336.2 1.6 collective-permute-start.10
  338.3 1.8 bitcast_dynamic-update-slice_fusion.15
  346.0 1.6 collective-permute-start.11
  354.7 1.8 bitcast_dynamic-update-slice_fusion.7
  374.2 1.8 collective-permute-start.14
  406.5 6.7 %collective-permute-done.17.rest_6_ = bf16[208,768]{1,0:T(8,128)(2,1)S(1)} collective-permute-done((bf16[208,768]{1,0:T(8,128)(2,1)S(1)}, bf16[208,768]{1,0:T(8,128)(2,1)S(1)}, u32[]{:S(2)}, u32[]{:S(2)}) %collective-permute-start.17) | collective-permute-done | bytes 319520 | tf_op jit(solution)/shard_map/ppermute | solution.py:595
  416.3 3.9 collective-permute-done.18.rest_7_
  423.6 3.4 maximum_select_fusion
  428.5 5.6 %unpack.5 = f32[3072,768]{1,0:T(8,128)} custom-call(s32[2]{0:T(128)} %pad_add_fusion.place, bf16[192,768]{1,0:T(8,128)(2,1)} %copy-done.28, bf16[192,768]{1,0:T(8,128)(2,1)} %copy-done.14, bf16[192,768]{1,0:T(8,128)(2,1)} %copy-done.17, bf16[192,768]{1,0:T(8,128)(2,1)} %copy-done.19, bf16[192,768]{1,0:T(8,128)(2,1)} %copy-done.21, ...), custom_call_target="tpu_custom_call" | custom-call | bytes 14155776 | tf_op jit(solution)/shard_map/unpack/pallas_call | solution.py:550
  434.1 5.6 %unpack.4 = f32[768,3072]{1,0:T(8,128)} custom-call(s32[2]{0:T(128)} %pad_add_fusion.place, bf16[192,768]{1,0:T(8,128)(2,1)} %copy-done.29, bf16[192,768]{1,0:T(8,128)(2,1)} %copy-done.15, bf16[192,768]{1,0:T(8,128)(2,1)} %copy-done.16, bf16[192,768]{1,0:T(8,128)(2,1)} %copy-done.18, bf16[192,768]{1,0:T(8,128)(2,1)} %copy-done.20, ...), custom_call_target="tpu_custom_call" | custom-call | bytes 14155776 | tf_op jit(solution)/shard_map/unpack/pallas_call | solution.py:550
  441.1 6.2 %unpack.3 = (f32[768,768]{1,0:T(8,128)}, f32[768,768]{1,0:T(8,128)}, f32[768,768]{1,0:T(8,128)}, f32[768,768]{1,0:T(8,128)}, f32[1,768]{1,0:T(1,128)}, /*index=5...) custom-call(s32[2]{0:T(128)} %pad_add_fusion.place, ...), custom_call_target="tpu_custom_call" | custom-call | bytes 15335424 | tf_op jit(solution)/shard_map/unpack/pallas_call | solution.py:550
  (202 shorter events, 113.1 us)
Async XLA Ops:
  29.5 30.8 %collective-permute-start = (bf16[512,768]{1,0:T(8,128)(2,1)}, bf16[512,768]{1,0:T(8,128)(2,1)S(1)}, u32[]{:S(2)}, u32[]{:S(2)}) collective-permute-start(bf16[512,768]{1,0:T(8,128)(2,1)} %get-tuple-element.138), channel_id=1, source_target_pairs={{0,16},{1,17},{2,18},{3,19},{4,20},{5,21},{6,22},{7,23},{8,24},{9,... | collective-permute-start | bytes 2359304 | tf_op jit(solution)/shard_map/ppermute | solution.py:617
  59.0 19.3 %collective-permute-start.1 = (bf16[512,768]{1,0:T(8,128)(2,1)}, bf16[512,768]{1,0:T(8,128)(2,1)S(1)}, u32[]{:S(2)}, u32[]{:S(2)}) collective-permute-start(bf16[512,768]{1,0:T(8,128)(2,1)} %get-tuple-element.140), channel_id=1, source_target_pairs={{0,16},{1,17},{2,18},{3,19},{4,20},{5,21},{6,22},{7,23},{8,24},{9,... | collective-permute-start | bytes 2359304 | tf_op jit(solution)/shard_map/ppermute | solution.py:619
  70.3 60.8 %collective-permute-start.2 = (bf16[512,768]{1,0:T(8,128)(2,1)}, bf16[512,768]{1,0:T(8,128)(2,1)S(1)}, u32[]{:S(2)}, u32[]{:S(2)}) collective-permute-start(bf16[512,768]{1,0:T(8,128)(2,1)} %get-tuple-element.169), channel_id=1, source_target_pairs={{16,0},{17,1},{18,2},{19,3},{20,4},{21,5},{22,6},{23,7},{24,8},{25... | collective-permute-start | bytes 2359304 | tf_op jit(solution)/shard_map/ppermute | solution.py:623
  166.2 29.8 %collective-permute-start.3 = (bf16[512,768]{1,0:T(8,128)(2,1)}, bf16[512,768]{1,0:T(8,128)(2,1)S(1)}, u32[]{:S(2)}, u32[]{:S(2)}) collective-permute-start(bf16[512,768]{1,0:T(8,128)(2,1)} %get-tuple-element.210), channel_id=1, source_target_pairs={{16,0},{17,1},{18,2},{19,3},{20,4},{21,5},{22,6},{23,7},{24,8},{25... | collective-permute-start | bytes 2359304 | tf_op jit(solution)/shard_map/ppermute | solution.py:629
  216.8 50.4 %collective-permute-start.36 = (bf16[6,256,768]{2,1,0:T(8,128)(2,1)}, bf16[6,256,768]{2,1,0:T(8,128)(2,1)}, u32[]{:S(2)}, u32[]{:S(2)}) collective-permute-start(bf16[6,256,768]{2,1,0:T(8,128)(2,1)} %weight_gradient.6), channel_id=1, source_target_pairs={{0,1},{1,0},{2,3},{3,2},{4,5},{5,4},{6,7},{7,6},{8,9},{9,8},{10,11... | collective-permute-start | bytes 7077896 | tf_op jit(solution)/shard_map/ppermute | solution.py:651
  224.5 45.6 %collective-permute-start.20 = (bf16[6,256,768]{2,1,0:T(8,128)(2,1)}, bf16[6,256,768]{2,1,0:T(8,128)(2,1)S(1)}, u32[]{:S(2)}, u32[]{:S(2)}) collective-permute-start(bf16[6,256,768]{2,1,0:T(8,128)(2,1)} %weight_gradient.4), channel_id=1, source_target_pairs={{0,1},{1,0},{2,3},{3,2},{4,5},{5,4},{6,7},{7,6},{8,9},{9,8},{10,11... | collective-permute-start | bytes 7077896 | tf_op jit(solution)/shard_map/ppermute | solution.py:651
  251.9 35.1 %collective-permute-start.4 = (bf16[8,208,768]{2,1,0:T(8,128)(2,1)}, bf16[8,208,768]{2,1,0:T(8,128)(2,1)}, u32[]{:S(2)}, u32[]{:S(2)}) collective-permute-start(bf16[8,208,768]{2,1,0:T(8,128)(2,1)} %attention_weight_gradient.2), channel_id=1, source_target_pairs={{0,1},{1,0},{2,3},{3,2},{4,5},{5,4},{6,7},{7,6},{8,9},{9,8},{10,11... | collective-permute-start | bytes 7667720 | tf_op jit(solution)/shard_map/ppermute | solution.py:651
  268.2 13.3 %collective-permute-start.37 = (bf16[192,768]{1,0:T(8,128)(2,1)S(1)}, bf16[192,768]{1,0:T(8,128)(2,1)S(1)}, u32[]{:S(2)}, u32[]{:S(2)}) collective-permute-start(bf16[192,768]{1,0:T(8,128)(2,1)S(1)} %add_bitcast_fusion.1), channel_id=1, source_target_pairs={{0,4},{1,3},{4,8},{5,1},{8,12},{9,5},{12,14},{13,9},{14,10},{15,13... | collective-permute-start | bytes 884744 | tf_op jit(solution)/shard_map/ppermute | solution.py:592
  272.5 12.0 %collective-permute-start.21 = (bf16[192,768]{1,0:T(8,128)(2,1)S(1)}, bf16[192,768]{1,0:T(8,128)(2,1)S(1)}, u32[]{:S(2)}, u32[]{:S(2)}) collective-permute-start(bf16[192,768]{1,0:T(8,128)(2,1)S(1)} %add_bitcast_fusion.2), channel_id=1, source_target_pairs={{0,4},{1,3},{4,8},{5,1},{8,12},{9,5},{12,14},{13,9},{14,10},{15,13... | collective-permute-start | bytes 884744 | tf_op jit(solution)/shard_map/ppermute | solution.py:592
  288.2 8.0 %collective-permute-start.5 = (bf16[208,768]{1,0:T(8,128)(2,1)S(1)}, bf16[208,768]{1,0:T(8,128)(2,1)S(1)}, u32[]{:S(2)}, u32[]{:S(2)}) collective-permute-start(bf16[208,768]{1,0:T(8,128)(2,1)S(1)} %add_bitcast_fusion), channel_id=1, source_target_pairs={{0,4},{1,3},{4,8},{5,1},{8,12},{9,5},{12,14},{13,9},{14,10},{15,13... | collective-permute-start | bytes 958472 | tf_op jit(solution)/shard_map/ppermute | solution.py:592
  290.7 8.7 %collective-permute-start.39 = (bf16[192,768]{1,0:T(8,128)(2,1)S(1)}, bf16[192,768]{1,0:T(8,128)(2,1)S(1)}, u32[]{:S(2)}, u32[]{:S(2)}) collective-permute-start(bf16[192,768]{1,0:T(8,128)(2,1)S(1)} %bitcast_add_fusion.12), channel_id=1, source_target_pairs={{0,4},{1,3},{4,8},{5,1},{8,12},{9,5},{12,14},{13,9},{14,10},{15,13... | collective-permute-start | bytes 884744 | tf_op jit(solution)/shard_map/ppermute | solution.py:592
  293.8 8.7 %collective-permute-start.23 = (bf16[192,768]{1,0:T(8,128)(2,1)S(1)}, bf16[192,768]{1,0:T(8,128)(2,1)S(1)}, u32[]{:S(2)}, u32[]{:S(2)}) collective-permute-start(bf16[192,768]{1,0:T(8,128)(2,1)S(1)} %bitcast_add_fusion.19), channel_id=1, source_target_pairs={{0,4},{1,3},{4,8},{5,1},{8,12},{9,5},{12,14},{13,9},{14,10},{15,13... | collective-permute-start | bytes 884744 | tf_op jit(solution)/shard_map/ppermute | solution.py:592
  297.3 8.7 %collective-permute-start.6 = (bf16[208,768]{1,0:T(8,128)(2,1)S(1)}, bf16[208,768]{1,0:T(8,128)(2,1)S(1)}, u32[]{:S(2)}, u32[]{:S(2)}) collective-permute-start(bf16[208,768]{1,0:T(8,128)(2,1)S(1)} %bitcast_add_fusion.6), channel_id=1, source_target_pairs={{0,4},{1,3},{4,8},{5,1},{8,12},{9,5},{12,14},{13,9},{14,10},{15,13... | collective-permute-start | bytes 958472 | tf_op jit(solution)/shard_map/ppermute | solution.py:592
  300.4 8.7 %collective-permute-start.40 = (bf16[192,768]{1,0:T(8,128)(2,1)S(1)}, bf16[192,768]{1,0:T(8,128)(2,1)S(1)}, u32[]{:S(2)}, u32[]{:S(2)}) collective-permute-start(bf16[192,768]{1,0:T(8,128)(2,1)S(1)} %bitcast_add_fusion.11), channel_id=1, source_target_pairs={{0,4},{1,3},{4,8},{5,1},{8,12},{9,5},{12,14},{13,9},{14,10},{15,13... | collective-permute-start | bytes 884744 | tf_op jit(solution)/shard_map/ppermute | solution.py:592
  302.6 9.7 %collective-permute-start.24 = (bf16[192,768]{1,0:T(8,128)(2,1)S(1)}, bf16[192,768]{1,0:T(8,128)(2,1)S(1)}, u32[]{:S(2)}, u32[]{:S(2)}) collective-permute-start(bf16[192,768]{1,0:T(8,128)(2,1)S(1)} %bitcast_add_fusion.18), channel_id=1, source_target_pairs={{0,4},{1,3},{4,8},{5,1},{8,12},{9,5},{12,14},{13,9},{14,10},{15,13... | collective-permute-start | bytes 884744 | tf_op jit(solution)/shard_map/ppermute | solution.py:592
  307.0 8.7 %collective-permute-start.7 = (bf16[208,768]{1,0:T(8,128)(2,1)S(1)}, bf16[208,768]{1,0:T(8,128)(2,1)S(1)}, u32[]{:S(2)}, u32[]{:S(2)}) collective-permute-start(bf16[208,768]{1,0:T(8,128)(2,1)S(1)} %bitcast_add_fusion.5), channel_id=1, source_target_pairs={{0,4},{1,3},{4,8},{5,1},{8,12},{9,5},{12,14},{13,9},{14,10},{15,13... | collective-permute-start | bytes 958472 | tf_op jit(solution)/shard_map/ppermute | solution.py:592
  310.1 8.7 %collective-permute-start.41 = (bf16[192,768]{1,0:T(8,128)(2,1)S(1)}, bf16[192,768]{1,0:T(8,128)(2,1)S(1)}, u32[]{:S(2)}, u32[]{:S(2)}) collective-permute-start(bf16[192,768]{1,0:T(8,128)(2,1)S(1)} %bitcast_add_fusion.10), channel_id=1, source_target_pairs={{0,4},{1,3},{4,8},{5,1},{8,12},{9,5},{12,14},{13,9},{14,10},{15,13... | collective-permute-start | bytes 884744 | tf_op jit(solution)/shard_map/ppermute | solution.py:592
  312.3 9.7 %collective-permute-start.25 = (bf16[192,768]{1,0:T(8,128)(2,1)S(1)}, bf16[192,768]{1,0:T(8,128)(2,1)S(1)}, u32[]{:S(2)}, u32[]{:S(2)}) collective-permute-start(bf16[192,768]{1,0:T(8,128)(2,1)S(1)} %bitcast_add_fusion.17), channel_id=1, source_target_pairs={{0,4},{1,3},{4,8},{5,1},{8,12},{9,5},{12,14},{13,9},{14,10},{15,13... | collective-permute-start | bytes 884744 | tf_op jit(solution)/shard_map/ppermute | solution.py:592
  316.7 8.7 %collective-permute-start.8 = (bf16[208,768]{1,0:T(8,128)(2,1)S(1)}, bf16[208,768]{1,0:T(8,128)(2,1)S(1)}, u32[]{:S(2)}, u32[]{:S(2)}) collective-permute-start(bf16[208,768]{1,0:T(8,128)(2,1)S(1)} %bitcast_add_fusion.4), channel_id=1, source_target_pairs={{0,4},{1,3},{4,8},{5,1},{8,12},{9,5},{12,14},{13,9},{14,10},{15,13... | collective-permute-start | bytes 958472 | tf_op jit(solution)/shard_map/ppermute | solution.py:592
  319.9 8.7 %collective-permute-start.42 = (bf16[192,768]{1,0:T(8,128)(2,1)S(1)}, bf16[192,768]{1,0:T(8,128)(2,1)S(1)}, u32[]{:S(2)}, u32[]{:S(2)}) collective-permute-start(bf16[192,768]{1,0:T(8,128)(2,1)S(1)} %bitcast_add_fusion.9), channel_id=1, source_target_pairs={{0,4},{1,3},{4,8},{5,1},{8,12},{9,5},{12,14},{13,9},{14,10},{15,13... | collective-permute-start | bytes 884744 | tf_op jit(solution)/shard_map/ppermute | solution.py:592
  322.1 9.7 %collective-permute-start.26 = (bf16[192,768]{1,0:T(8,128)(2,1)S(1)}, bf16[192,768]{1,0:T(8,128)(2,1)S(1)}, u32[]{:S(2)}, u32[]{:S(2)}) collective-permute-start(bf16[192,768]{1,0:T(8,128)(2,1)S(1)} %bitcast_add_fusion.16), channel_id=1, source_target_pairs={{0,4},{1,3},{4,8},{5,1},{8,12},{9,5},{12,14},{13,9},{14,10},{15,13... | collective-permute-start | bytes 884744 | tf_op jit(solution)/shard_map/ppermute | solution.py:592
  326.5 8.7 %collective-permute-start.9 = (bf16[208,768]{1,0:T(8,128)(2,1)S(1)}, bf16[208,768]{1,0:T(8,128)(2,1)S(1)}, u32[]{:S(2)}, u32[]{:S(2)}) collective-permute-start(bf16[208,768]{1,0:T(8,128)(2,1)S(1)} %bitcast_add_fusion.3), channel_id=1, source_target_pairs={{0,4},{1,3},{4,8},{5,1},{8,12},{9,5},{12,14},{13,9},{14,10},{15,13... | collective-permute-start | bytes 958472 | tf_op jit(solution)/shard_map/ppermute | solution.py:592
  329.6 8.7 %collective-permute-start.43 = (bf16[192,768]{1,0:T(8,128)(2,1)S(1)}, bf16[192,768]{1,0:T(8,128)(2,1)S(1)}, u32[]{:S(2)}, u32[]{:S(2)}) collective-permute-start(bf16[192,768]{1,0:T(8,128)(2,1)S(1)} %bitcast_add_fusion.8), channel_id=1, source_target_pairs={{0,4},{1,3},{4,8},{5,1},{8,12},{9,5},{12,14},{13,9},{14,10},{15,13... | collective-permute-start | bytes 884744 | tf_op jit(solution)/shard_map/ppermute | solution.py:592
  331.8 9.9 %collective-permute-start.27 = (bf16[192,768]{1,0:T(8,128)(2,1)S(1)}, bf16[192,768]{1,0:T(8,128)(2,1)S(1)}, u32[]{:S(2)}, u32[]{:S(2)}) collective-permute-start(bf16[192,768]{1,0:T(8,128)(2,1)S(1)} %bitcast_add_fusion.15), channel_id=1, source_target_pairs={{0,4},{1,3},{4,8},{5,1},{8,12},{9,5},{12,14},{13,9},{14,10},{15,13... | collective-permute-start | bytes 884744 | tf_op jit(solution)/shard_map/ppermute | solution.py:592
  336.2 8.7 %collective-permute-start.10 = (bf16[208,768]{1,0:T(8,128)(2,1)S(1)}, bf16[208,768]{1,0:T(8,128)(2,1)S(1)}, u32[]{:S(2)}, u32[]{:S(2)}) collective-permute-start(bf16[208,768]{1,0:T(8,128)(2,1)S(1)} %bitcast_add_fusion.2), channel_id=1, source_target_pairs={{0,4},{1,3},{4,8},{5,1},{8,12},{9,5},{12,14},{13,9},{14,10},{15,13... | collective-permute-start | bytes 958472 | tf_op jit(solution)/shard_map/ppermute | solution.py:592
  340.1 7.9 %collective-permute-start.44 = (bf16[192,768]{1,0:T(8,128)(2,1)S(1)}, bf16[192,768]{1,0:T(8,128)(2,1)S(1)}, u32[]{:S(2)}, u32[]{:S(2)}) collective-permute-start(bf16[192,768]{1,0:T(8,128)(2,1)S(1)} %get-tuple-element.260.rest_0_), channel_id=1, source_target_pairs={{0,4},{1,3},{4,8},{5,1},{8,12},{9,5},{12,14},{13,9},{14,10},{15,13... | collective-permute-start | bytes 884744 | tf_op jit(solution)/shard_map/ppermute | solution.py:595
  342.6 8.7 %collective-permute-start.28 = (bf16[192,768]{1,0:T(8,128)(2,1)S(1)}, bf16[192,768]{1,0:T(8,128)(2,1)S(1)}, u32[]{:S(2)}, u32[]{:S(2)}) collective-permute-start(bf16[192,768]{1,0:T(8,128)(2,1)S(1)} %get-tuple-element.262.rest_0_), channel_id=1, source_target_pairs={{0,4},{1,3},{4,8},{5,1},{8,12},{9,5},{12,14},{13,9},{14,10},{15,13... | collective-permute-start | bytes 884744 | tf_op jit(solution)/shard_map/ppermute | solution.py:595
  346.0 8.7 %collective-permute-start.11 = (bf16[208,768]{1,0:T(8,128)(2,1)S(1)}, bf16[208,768]{1,0:T(8,128)(2,1)S(1)}, u32[]{:S(2)}, u32[]{:S(2)}) collective-permute-start(bf16[208,768]{1,0:T(8,128)(2,1)S(1)} %bitcast_add_fusion.1), channel_id=1, source_target_pairs={{0,4},{1,3},{4,8},{5,1},{8,12},{9,5},{12,14},{13,9},{14,10},{15,13... | collective-permute-start | bytes 958472 | tf_op jit(solution)/shard_map/ppermute | solution.py:592
  348.1 10.0 %collective-permute-start.45 = (bf16[192,768]{1,0:T(8,128)(2,1)S(1)}, bf16[192,768]{1,0:T(8,128)(2,1)S(1)}, u32[]{:S(2)}, u32[]{:S(2)}) collective-permute-start(bf16[192,768]{1,0:T(8,128)(2,1)S(1)} %collective-permute-done.44.rest_1_), channel_id=1, source_target_pairs={{0,4},{1,3},{4,8},{5,1},{8,12},{9,5},{12,14},{13,9},{14,10},{15,13... | collective-permute-start | bytes 884744 | tf_op jit(solution)/shard_map/ppermute | solution.py:595
  351.2 9.7 %collective-permute-start.29 = (bf16[192,768]{1,0:T(8,128)(2,1)S(1)}, bf16[192,768]{1,0:T(8,128)(2,1)S(1)}, u32[]{:S(2)}, u32[]{:S(2)}) collective-permute-start(bf16[192,768]{1,0:T(8,128)(2,1)S(1)} %collective-permute-done.28.rest_1_), channel_id=1, source_target_pairs={{0,4},{1,3},{4,8},{5,1},{8,12},{9,5},{12,14},{13,9},{14,10},{15,13... | collective-permute-start | bytes 884744 | tf_op jit(solution)/shard_map/ppermute | solution.py:595
  358.1 9.5 %collective-permute-start.46 = (bf16[192,768]{1,0:T(8,128)(2,1)S(1)}, bf16[192,768]{1,0:T(8,128)(2,1)S(1)}, u32[]{:S(2)}, u32[]{:S(2)}) collective-permute-start(bf16[192,768]{1,0:T(8,128)(2,1)S(1)} %collective-permute-done.45.rest_2_), channel_id=1, source_target_pairs={{0,4},{1,3},{4,8},{5,1},{8,12},{9,5},{12,14},{13,9},{14,10},{15,13... | collective-permute-start | bytes 884744 | tf_op jit(solution)/shard_map/ppermute | solution.py:595
  361.0 9.7 %collective-permute-start.30 = (bf16[192,768]{1,0:T(8,128)(2,1)S(1)}, bf16[192,768]{1,0:T(8,128)(2,1)S(1)}, u32[]{:S(2)}, u32[]{:S(2)}) collective-permute-start(bf16[192,768]{1,0:T(8,128)(2,1)S(1)} %collective-permute-done.29.rest_2_), channel_id=1, source_target_pairs={{0,4},{1,3},{4,8},{5,1},{8,12},{9,5},{12,14},{13,9},{14,10},{15,13... | collective-permute-start | bytes 884744 | tf_op jit(solution)/shard_map/ppermute | solution.py:595
  364.4 9.7 %collective-permute-start.13 = (bf16[208,768]{1,0:T(8,128)(2,1)S(1)}, bf16[208,768]{1,0:T(8,128)(2,1)S(1)}, u32[]{:S(2)}, u32[]{:S(2)}) collective-permute-start(bf16[208,768]{1,0:T(8,128)(2,1)S(1)} %collective-permute-done.12.rest_1_), channel_id=1, source_target_pairs={{0,4},{1,3},{4,8},{5,1},{8,12},{9,5},{12,14},{13,9},{14,10},{15,13... | collective-permute-start | bytes 958472 | tf_op jit(solution)/shard_map/ppermute | solution.py:595
  367.6 9.7 %collective-permute-start.47 = (bf16[192,768]{1,0:T(8,128)(2,1)S(1)}, bf16[192,768]{1,0:T(8,128)(2,1)S(1)}, u32[]{:S(2)}, u32[]{:S(2)}) collective-permute-start(bf16[192,768]{1,0:T(8,128)(2,1)S(1)} %collective-permute-done.46.rest_3_), channel_id=1, source_target_pairs={{0,4},{1,3},{4,8},{5,1},{8,12},{9,5},{12,14},{13,9},{14,10},{15,13... | collective-permute-start | bytes 884744 | tf_op jit(solution)/shard_map/ppermute | solution.py:595
  370.7 9.7 %collective-permute-start.31 = (bf16[192,768]{1,0:T(8,128)(2,1)S(1)}, bf16[192,768]{1,0:T(8,128)(2,1)S(1)}, u32[]{:S(2)}, u32[]{:S(2)}) collective-permute-start(bf16[192,768]{1,0:T(8,128)(2,1)S(1)} %collective-permute-done.30.rest_3_), channel_id=1, source_target_pairs={{0,4},{1,3},{4,8},{5,1},{8,12},{9,5},{12,14},{13,9},{14,10},{15,13... | collective-permute-start | bytes 884744 | tf_op jit(solution)/shard_map/ppermute | solution.py:595
  374.2 9.7 %collective-permute-start.14 = (bf16[208,768]{1,0:T(8,128)(2,1)S(1)}, bf16[208,768]{1,0:T(8,128)(2,1)S(1)}, u32[]{:S(2)}, u32[]{:S(2)}) collective-permute-start(bf16[208,768]{1,0:T(8,128)(2,1)S(1)} %collective-permute-done.13.rest_2_), channel_id=1, source_target_pairs={{0,4},{1,3},{4,8},{5,1},{8,12},{9,5},{12,14},{13,9},{14,10},{15,13... | collective-permute-start | bytes 958472 | tf_op jit(solution)/shard_map/ppermute | solution.py:595
  377.3 9.7 %collective-permute-start.48 = (bf16[192,768]{1,0:T(8,128)(2,1)S(1)}, bf16[192,768]{1,0:T(8,128)(2,1)S(1)}, u32[]{:S(2)}, u32[]{:S(2)}) collective-permute-start(bf16[192,768]{1,0:T(8,128)(2,1)S(1)} %collective-permute-done.47.rest_4_), channel_id=1, source_target_pairs={{0,4},{1,3},{4,8},{5,1},{8,12},{9,5},{12,14},{13,9},{14,10},{15,13... | collective-permute-start | bytes 884744 | tf_op jit(solution)/shard_map/ppermute | solution.py:595
  380.5 9.7 %collective-permute-start.32 = (bf16[192,768]{1,0:T(8,128)(2,1)S(1)}, bf16[192,768]{1,0:T(8,128)(2,1)S(1)}, u32[]{:S(2)}, u32[]{:S(2)}) collective-permute-start(bf16[192,768]{1,0:T(8,128)(2,1)S(1)} %collective-permute-done.31.rest_4_), channel_id=1, source_target_pairs={{0,4},{1,3},{4,8},{5,1},{8,12},{9,5},{12,14},{13,9},{14,10},{15,13... | collective-permute-start | bytes 884744 | tf_op jit(solution)/shard_map/ppermute | solution.py:595
  383.9 9.7 %collective-permute-start.15 = (bf16[208,768]{1,0:T(8,128)(2,1)S(1)}, bf16[208,768]{1,0:T(8,128)(2,1)S(1)}, u32[]{:S(2)}, u32[]{:S(2)}) collective-permute-start(bf16[208,768]{1,0:T(8,128)(2,1)S(1)} %collective-permute-done.14.rest_3_), channel_id=1, source_target_pairs={{0,4},{1,3},{4,8},{5,1},{8,12},{9,5},{12,14},{13,9},{14,10},{15,13... | collective-permute-start | bytes 958472 | tf_op jit(solution)/shard_map/ppermute | solution.py:595
  387.1 9.7 %collective-permute-start.49 = (bf16[192,768]{1,0:T(8,128)(2,1)S(1)}, bf16[192,768]{1,0:T(8,128)(2,1)S(1)}, u32[]{:S(2)}, u32[]{:S(2)}) collective-permute-start(bf16[192,768]{1,0:T(8,128)(2,1)S(1)} %collective-permute-done.48.rest_5_), channel_id=1, source_target_pairs={{0,4},{1,3},{4,8},{5,1},{8,12},{9,5},{12,14},{13,9},{14,10},{15,13... | collective-permute-start | bytes 884744 | tf_op jit(solution)/shard_map/ppermute | solution.py:595
  390.2 9.7 %collective-permute-start.33 = (bf16[192,768]{1,0:T(8,128)(2,1)S(1)}, bf16[192,768]{1,0:T(8,128)(2,1)S(1)}, u32[]{:S(2)}, u32[]{:S(2)}) collective-permute-start(bf16[192,768]{1,0:T(8,128)(2,1)S(1)} %collective-permute-done.32.rest_5_), channel_id=1, source_target_pairs={{0,4},{1,3},{4,8},{5,1},{8,12},{9,5},{12,14},{13,9},{14,10},{15,13... | collective-permute-start | bytes 884744 | tf_op jit(solution)/shard_map/ppermute | solution.py:595
  393.6 9.7 %collective-permute-start.16 = (bf16[208,768]{1,0:T(8,128)(2,1)S(1)}, bf16[208,768]{1,0:T(8,128)(2,1)S(1)}, u32[]{:S(2)}, u32[]{:S(2)}) collective-permute-start(bf16[208,768]{1,0:T(8,128)(2,1)S(1)} %collective-permute-done.15.rest_4_), channel_id=1, source_target_pairs={{0,4},{1,3},{4,8},{5,1},{8,12},{9,5},{12,14},{13,9},{14,10},{15,13... | collective-permute-start | bytes 958472 | tf_op jit(solution)/shard_map/ppermute | solution.py:595
  396.8 17.9 %collective-permute-start.50 = (bf16[192,768]{1,0:T(8,128)(2,1)S(1)}, bf16[192,768]{1,0:T(8,128)(2,1)S(1)}, u32[]{:S(2)}, u32[]{:S(2)}) collective-permute-start(bf16[192,768]{1,0:T(8,128)(2,1)S(1)} %collective-permute-done.49.rest_6_), channel_id=1, source_target_pairs={{0,4},{1,3},{4,8},{5,1},{8,12},{9,5},{12,14},{13,9},{14,10},{15,13... | collective-permute-start | bytes 884744 | tf_op jit(solution)/shard_map/ppermute | solution.py:595
  400.0 21.7 %collective-permute-start.34 = (bf16[192,768]{1,0:T(8,128)(2,1)S(1)}, bf16[192,768]{1,0:T(8,128)(2,1)S(1)}, u32[]{:S(2)}, u32[]{:S(2)}) collective-permute-start(bf16[192,768]{1,0:T(8,128)(2,1)S(1)} %collective-permute-done.33.rest_6_), channel_id=1, source_target_pairs={{0,4},{1,3},{4,8},{5,1},{8,12},{9,5},{12,14},{13,9},{14,10},{15,13... | collective-permute-start | bytes 884744 | tf_op jit(solution)/shard_map/ppermute | solution.py:595
  403.4 9.7 %collective-permute-start.17 = (bf16[208,768]{1,0:T(8,128)(2,1)S(1)}, bf16[208,768]{1,0:T(8,128)(2,1)S(1)}, u32[]{:S(2)}, u32[]{:S(2)}) collective-permute-start(bf16[208,768]{1,0:T(8,128)(2,1)S(1)} %collective-permute-done.16.rest_5_), channel_id=1, source_target_pairs={{0,4},{1,3},{4,8},{5,1},{8,12},{9,5},{12,14},{13,9},{14,10},{15,13... | collective-permute-start | bytes 958472 | tf_op jit(solution)/shard_map/ppermute | solution.py:595
  415.5 13.0 %collective-permute-start.51 = (bf16[8,192,768]{2,1,0:T(8,128)(2,1)}, bf16[8,192,768]{2,1,0:T(8,128)(2,1)}, u32[]{:S(2)}, u32[]{:S(2)}) collective-permute-start(bf16[8,192,768]{2,1,0:T(8,128)(2,1)} %bitcast_dynamic-update-slice_fusion.8), channel_id=1, source_target_pairs={{0,1},{1,0},{2,3},{3,2},{4,5},{5,4},{6,7},{7,6},{8,9},{9,8},{10,11... | collective-permute-start | bytes 7077896 | tf_op jit(solution)/shard_map/ppermute | solution.py:655
  421.6 18.0 %collective-permute-start.19 = (bf16[8,208,768]{2,1,0:T(8,128)(2,1)}, bf16[8,208,768]{2,1,0:T(8,128)(2,1)S(1)}, u32[]{:S(2)}, u32[]{:S(2)}) collective-permute-start(bf16[8,208,768]{2,1,0:T(8,128)(2,1)} %bitcast_dynamic-update-slice_fusion), channel_id=1, source_target_pairs={{0,1},{1,0},{2,3},{3,2},{4,5},{5,4},{6,7},{7,6},{8,9},{9,8},{10,11... | collective-permute-start | bytes 7667720 | tf_op jit(solution)/shard_map/ppermute | solution.py:655
  422.5 11.6 %collective-permute-start.35 = (bf16[8,192,768]{2,1,0:T(8,128)(2,1)}, bf16[8,192,768]{2,1,0:T(8,128)(2,1)}, u32[]{:S(2)}, u32[]{:S(2)}) collective-permute-start(bf16[8,192,768]{2,1,0:T(8,128)(2,1)} %bitcast_dynamic-update-slice_fusion.16), channel_id=1, source_target_pairs={{0,1},{1,0},{2,3},{3,2},{4,5},{5,4},{6,7},{7,6},{8,9},{9,8},{10,11... | collective-permute-start | bytes 7077896 | tf_op jit(solution)/shard_map/ppermute | solution.py:655
  (42 other events, 593.2 us)
